TPU v7x, 32 devices: a whole 2x2x4 slice. The times are simulated.
32 devices in a mesh: gx: 2 (over x), gy: 4 (over y, core), gz: 4 (over z).
Axes of the slice: x: 2, y: 2, z: 4, core: 2. Of those that a mesh axis runs over, the one named last changes fastest.
Arguments:
- right_side: float32 [32, 256, 512], P('gx', 'gz', 'gy'), may hold values from -8 to 8, as said below
- absorption: float32 [32, 256, 512], P('gx', 'gz', 'gy'), may hold values from 1e-05 to 1, as said below
Outputs:
- fine_iterate: float32 [32, 256, 512], P('gx', 'gz', 'gy')
- middle_iterate: float32 [16, 128, 256], P('gx', 'gz', 'gy')
- corrected_iterate: float32 [8, 64, 128], P('gx', 'gz', 'gy')
Inputs may be any that keep to these rules, and one draw needn't show every extreme that they name: `right_side`: independent cell values, possibly with a smooth part added. `absorption`: positive at every cell.
All inputs are finite; a program needn't handle non-finite values.
Results may differ from a plain program's by a relative error of at most 0.0001.
Values sent between devices are 32-bit elements; how exact they have to be, the bound alone decides.
A program may use at most 128 MiB of HBM per device.

v0:
```python
import jax
import jax.numpy as jnp
from jax import lax
from jax.sharding import PartitionSpec as P

DEGREE = 4
LEVELS = 3
BOTTOM_ITERS = 20


smooth_low = 1.5
smooth_top = 12.0
absorb_top = 1.0
bottom_low = 0.008


def extended_2(cells, sides, width):
    for axis, dim in sides:
        count = lax.axis_size(axis)
        ends = count - 1
        head = lax.slice_in_dim(cells, 0, width, axis=dim)
        tail = lax.slice_in_dim(cells, cells.shape[dim] - width, cells.shape[dim], axis=dim)
        cells = jnp.concatenate(
            [
                lax.ppermute(tail, axis, [(i, (i + 1) % count) for i in range(ends)]),
                cells,
                lax.ppermute(head, axis, [((i + 1) % count, i) for i in range(ends)]),
            ],
            axis=dim,
        )
    return cells


def from_partner(value, axis, bit):
    mask = 2**bit
    pairs = [(source, source ^ mask) for source in range(lax.axis_size(axis))]
    return lax.ppermute(value, axis, pairs)


def cheb_tables(count, lower, upper):
    theta = (upper + lower) / 2.0
    delta = (upper - lower) / 2.0
    sigma = theta / delta
    rho_value = 1.0 / sigma
    firsts = []
    seconds = []
    for turn_index in range(count - 1):
        rho_next = 1.0 / (2.0 * sigma - rho_value)
        firsts.append(rho_next * rho_value)
        seconds.append(2.0 * rho_next / delta)
        rho_value = rho_next
    return (1.0 / theta, firsts, seconds)


def chebyshev(source, coefficient, count, lower, upper, operate):
    start_scale, firsts, seconds = cheb_tables(count, lower, upper)
    first_table = jnp.asarray(firsts, jnp.float32)
    second_table = jnp.asarray(seconds, jnp.float32)
    direction = source * start_scale

    def turn(turn_index, carry):
        iterate, direction, residual = carry
        residual = residual - operate(direction, coefficient)
        direction = first_table[turn_index] * direction + second_table[turn_index] * residual
        return (iterate + direction, direction, residual)

    iterate, direction, residual = lax.fori_loop(0, count - 1, turn, (direction, direction, source))
    return iterate


def neighbours(padded):
    return (
        padded[2:, 1:-1, 1:-1]
        + padded[:-2, 1:-1, 1:-1]
        + padded[1:-1, 2:, 1:-1]
        + padded[1:-1, :-2, 1:-1]
        + padded[1:-1, 1:-1, 2:]
        + padded[1:-1, 1:-1, :-2]
    )


def thin_operator(field, coefficient):
    padded = extended_2(field, (("gx", 0), ("gy", 2), ("gz", 1)), 1)
    return (6.0 + coefficient) * field - neighbours(padded)


def restrict_four(field):
    first, second, third = field.shape
    blocks = field.reshape(first // 2, 2, second // 2, 2, third // 2, 2)
    return blocks.sum(axis=(1, 3, 5)) * 0.5


def prolong_axis(extended, axis):
    count = extended.shape[axis] - 2
    center = lax.slice_in_dim(extended, 1, count + 1, axis=axis)
    lower = lax.slice_in_dim(extended, 0, count, axis=axis)
    upper = lax.slice_in_dim(extended, 2, count + 2, axis=axis)
    even = 0.75 * center + 0.25 * lower
    odd = 0.75 * center + 0.25 * upper
    stacked = jnp.stack((even, odd), axis=axis + 1)
    shape = list(extended.shape)
    shape[axis] = 2 * count
    return stacked.reshape(shape)


def prolong(extended):
    for axis in range(3):
        extended = prolong_axis(extended, axis)
    return extended


def join_pair(mine, partner, index, bit, dim):
    upper_half = index // 2**bit % 2 == 1
    return jnp.where(
        upper_half, jnp.concatenate((partner, mine), dim), jnp.concatenate((mine, partner), dim)
    )


def extend_bottom(field):
    return jnp.pad(field, 1)


def bottom_operator(field, coefficient):
    return (6.0 + coefficient) * field - neighbours(extend_bottom(field))


def on_device(right_side, absorption):
    source = right_side
    coefficient = absorption
    iterates = []
    for section in range(LEVELS):
        upper_bound = smooth_top + 4.0**section * absorb_top
        iterate = chebyshev(source, coefficient, DEGREE + 1, smooth_low, upper_bound, thin_operator)
        padded = extended_2(iterate, (("gx", 0), ("gy", 2), ("gz", 1)), 1)
        residual = source - ((6.0 + coefficient) * iterate - neighbours(padded))
        iterates.append(iterate)
        source = restrict_four(residual)
        coefficient = restrict_four(coefficient)
    folded = jnp.stack((source, coefficient))
    for bit in range(lax.axis_size("gx").bit_length() - 1):
        partner = from_partner(folded, "gx", bit)
        folded = join_pair(folded, partner, lax.axis_index("gx"), bit, 1)
    for bit in range(lax.axis_size("gy").bit_length() - 1):
        partner = from_partner(folded, "gy", bit)
        folded = join_pair(folded, partner, lax.axis_index("gy"), bit, 3)
    for bit in range(lax.axis_size("gz").bit_length() - 1):
        partner = from_partner(folded, "gz", bit)
        folded = join_pair(folded, partner, lax.axis_index("gz"), bit, 2)
    bottom_top = smooth_top + 4.0**LEVELS * absorb_top
    correction = chebyshev(
        folded[0], folded[1], BOTTOM_ITERS, bottom_low, bottom_top, bottom_operator
    )
    extended = extend_bottom(correction)
    block_first = source.shape[0]
    block_second = source.shape[1]
    block_third = source.shape[2]
    window = lax.dynamic_slice_in_dim(
        extended, lax.axis_index("gx") * block_first, block_first + 2, 0
    )
    window = lax.dynamic_slice_in_dim(
        window, lax.axis_index("gy") * block_third, block_third + 2, 2
    )
    window = lax.dynamic_slice_in_dim(
        window, lax.axis_index("gz") * block_second, block_second + 2, 1
    )
    corrected = iterates[2] + prolong(window)
    return (iterates[0], iterates[1], corrected)


def solution(mesh):
    placed = (P("gx", "gz", "gy"), P("gx", "gz", "gy"))
    return jax.shard_map(
        on_device,
        mesh=mesh,
        in_specs=placed,
        out_specs=(P("gx", "gz", "gy"), P("gx", "gz", "gy"), P("gx", "gz", "gy")),
        check_vma=False,
    )
```

profile of v0, /device:TPU:0, one launch (start us, length us, event | category | flops | bytes accessed | tf_op | source)
XLA Modules:
  0.0 630.6 jit_solution(2423788012169171671)
XLA Ops:
  8.0 163.6 %while.74 = (s32[]{:T(128)}, f32[16,64,128]{1,2,0:T(8,128)}, f32[16,64,128]{1,2,0:T(8,128)}, f32[16,64,128]{1,2,0:T(8,128)}, f32[16,64,128]{1,2,0:T(8,128)}, /*index=5*/s32[]{:T(128)}, f32[4]{0:T(128)S(1)}, f32[4]{0:T(128)S(1)}) while((s32[]{:T(128)}, f32[16,64,128]{1,2,0:T(8,128)}, f32[16,64,128]{1,2,0:T(8,128)}, ...), condition=%wide.region_1.0_spmd.clone, body=%wide.region_0.0_spmd.sunk.clone.sunk | while | flops 3314178 | bytes 9730593 | solution.py:67
  9.2 4.8 collective-permute-start
  16.0 4.2 collective-permute-done.1
  22.9 3.5 collective-permute-done.3
  31.1 4.1 collective-permute-start.4
  44.7 6.6 %fusion.100 = (f32[16,64,128]{1,2,0:T(8,128)}, f32[16,64,128]{1,2,0:T(8,128)}, f32[16,64,128]{1,2,0:T(8,128)}) fusion(f32[16,64,128]{1,2,0:T(8,128)} %get-tuple-element.951, f32[]{:T(128)} %bitcast.41, f32[16,64,128]{1,2,0:T(8,128)S(1)} %copy.129, f32[]{:T(128)} %bitcast.42, f32[16,64,128]{1,2,0:T(8,128)} %get-tuple-element.953, ...), kind=kLoop, calls=%fused_computation.196.clone.1 | loop fusion | flops 3014656 | bytes 4353320 | tf_op jit(solution)/shard_map/while/body/eval_jaxpr/add | solution.py:65
  56.6 4.1 collective-permute-done.1
  72.0 3.5 collective-permute-start.4
  85.0 6.6 %fusion.100 = (f32[16,64,128]{1,2,0:T(8,128)}, f32[16,64,128]{1,2,0:T(8,128)}, f32[16,64,128]{1,2,0:T(8,128)}) fusion(f32[16,64,128]{1,2,0:T(8,128)} %get-tuple-element.951, f32[]{:T(128)} %bitcast.41, f32[16,64,128]{1,2,0:T(8,128)S(1)} %copy.129, f32[]{:T(128)} %bitcast.42, f32[16,64,128]{1,2,0:T(8,128)} %get-tuple-element.953, ...), kind=kLoop, calls=%fused_computation.196.clone.1 | loop fusion | flops 3014656 | bytes 4353320 | tf_op jit(solution)/shard_map/while/body/eval_jaxpr/add | solution.py:65
  96.9 4.1 collective-permute-done.1
  112.3 3.5 collective-permute-start.4
  125.2 6.6 %fusion.100 = (f32[16,64,128]{1,2,0:T(8,128)}, f32[16,64,128]{1,2,0:T(8,128)}, f32[16,64,128]{1,2,0:T(8,128)}) fusion(f32[16,64,128]{1,2,0:T(8,128)} %get-tuple-element.951, f32[]{:T(128)} %bitcast.41, f32[16,64,128]{1,2,0:T(8,128)S(1)} %copy.129, f32[]{:T(128)} %bitcast.42, f32[16,64,128]{1,2,0:T(8,128)} %get-tuple-element.953, ...), kind=kLoop, calls=%fused_computation.196.clone.1 | loop fusion | flops 3014656 | bytes 4353320 | tf_op jit(solution)/shard_map/while/body/eval_jaxpr/add | solution.py:65
  137.2 4.1 collective-permute-done.1
  165.0 6.6 %fusion.100 = (f32[16,64,128]{1,2,0:T(8,128)}, f32[16,64,128]{1,2,0:T(8,128)}, f32[16,64,128]{1,2,0:T(8,128)}) fusion(f32[16,64,128]{1,2,0:T(8,128)} %get-tuple-element.951, f32[]{:T(128)} %bitcast.41, f32[16,64,128]{1,2,0:T(8,128)S(1)} %copy.129, f32[]{:T(128)} %bitcast.42, f32[16,64,128]{1,2,0:T(8,128)} %get-tuple-element.953, ...), kind=kLoop, calls=%fused_computation.196.clone.1 | loop fusion | flops 3014656 | bytes 4353320 | tf_op jit(solution)/shard_map/while/body/eval_jaxpr/add | solution.py:65
  183.7 3.4 collective-permute-done.21
  197.1 34.8 %reshape.54 = f32[8,2,32,2,64,2]{5,4,3,2,1,0:T(8,128)} reshape(f32[16,64,128]{2,1,0:T(8,128)S(1)} %copy-done.6) | data formatting | bytes 1048576 | tf_op jit(solution)/shard_map/reshape | solution.py:89
  231.9 12.2 %reduce_sum.55 = f32[8,32,64]{2,1,0:T(8,128)S(1)} reduce(f32[8,2,32,2,64,2]{5,4,3,2,1,0:T(8,128)} %reshape.54, f32[]{:T(128)} %constant.276.clone.1), dimensions={1,3,5}, to_apply=%region_3.0 | reduce | flops 114688 | bytes 589828 | tf_op jit(solution)/shard_map/reduce_sum | solution.py:90
  248.8 4.8 fusion.30
  255.1 34.8 %reshape.53 = f32[8,2,32,2,64,2]{5,4,3,2,1,0:T(8,128)} reshape(f32[16,64,128]{2,1,0:T(8,128)S(1)} %copy.49) | data formatting | bytes 1048576 | tf_op jit(solution)/shard_map/reshape | solution.py:89
  290.0 12.2 %reduce_sum.54 = f32[8,32,64]{2,1,0:T(8,128)S(1)} reduce(f32[8,2,32,2,64,2]{5,4,3,2,1,0:T(8,128)} %reshape.53, f32[]{:T(128)} %constant.276.clone.1), dimensions={1,3,5}, to_apply=%region_2.0 | reduce | flops 114688 | bytes 589828 | tf_op jit(solution)/shard_map/reduce_sum | solution.py:90
  302.3 103.3 %while.75 = (s32[]{:T(128)}, f32[8,32,64]{2,1,0:T(8,128)S(1)}, f32[8,32,64]{2,1,0:T(8,128)S(1)}, f32[8,32,64]{2,1,0:T(8,128)S(1)}, f32[8,32,64]{2,1,0:T(8,128)S(...) while((s32[]{:T(128)}, f32[8,32,64]{2,1,0:T(8,128)S(1)}, f32[8,32,64]{2,1,0:T(8,128)S(1)}, ...), condition=%wide.region_5.0_spmd.clone, body=%wide.region_4.0_spmd.sunk.clone.sunk | while | flops 379474 | bytes 1240365 | solution.py:67
  305.3 4.2 collective-permute-done.7
  316.9 4.5 collective-permute-start.10
  331.8 4.2 collective-permute-done.7
  340.3 4.2 collective-permute-done.9
  357.2 4.2 collective-permute-done.7
  365.7 4.2 collective-permute-done.9
  383.7 4.2 collective-permute-done.7
  392.2 4.2 collective-permute-done.9
  408.7 4.2 collective-permute-done.24
  417.2 5.7 mul.284
  429.3 4.2 collective-permute-done.28
  433.8 5.7 reshape.55
  442.1 96.0 %while.76 = (s32[]{:T(128)}, f32[4,16,32]{2,1,0:T(8,128)S(1)}, f32[4,16,32]{2,1,0:T(8,128)S(1)}, f32[4,16,32]{2,1,0:T(8,128)S(1)}, f32[4,16,32]{2,1,0:T(8,128)S(...) while((s32[]{:T(128)}, f32[4,16,32]{2,1,0:T(8,128)S(1)}, f32[4,16,32]{2,1,0:T(8,128)S(1)}, ...), condition=%wide.region_9.0_spmd.clone, body=%wide.region_8.0_spmd.sunk.clone.sunk | while | flops 47922 | bytes 235437 | solution.py:67
  445.4 4.2 collective-permute-done.13
  452.6 5.9 collective-permute-done.15
  470.5 4.2 collective-permute-done.13
  478.1 4.0 collective-permute-done.15
  494.1 4.2 collective-permute-done.13
  501.7 4.0 collective-permute-done.15
  517.6 4.2 collective-permute-done.13
  525.2 4.0 collective-permute-done.15
  541.2 4.2 collective-permute-done.30
  549.2 3.5 collective-permute-done.33
  556.1 4.2 collective-permute-done.34
  560.9 3.7 collective-permute-done.36
  570.8 3.9 collective-permute-done.39
  580.2 49.3 %while.77 = (s32[]{:T(128)}, f32[4,32,64]{2,1,0:T(8,128)S(1)}, f32[4,32,64]{2,1,0:T(8,128)S(1)}, f32[4,32,64]{2,1,0:T(8,128)S(1)}, f32[4,32,64]{2,1,0:T(8,128)S(...) while((s32[]{:T(128)}, f32[4,32,64]{2,1,0:T(8,128)S(1)}, ...), condition=%wide.region_13.14_spmd.clone, body=%wide.region_12.13_spmd.sunk.clone.sunk | while | flops 106498 | bytes 295037 | solution.py:67
  (489 shorter events, 355.6 us)
Async XLA Ops:
  9.2 6.7 %collective-permute-start = (f32[1,64,128]{1,2,0:T(8,128)S(1)}, f32[1,64,128]{1,2,0:T(8,128)S(1)}, u32[]{:S(2)}, u32[]{:S(2)}) collective-permute-start(f32[1,64,128]{1,2,0:T(8,128)S(1)} %get-tuple-element.897), channel_id=1, source_target_pairs={{0,16},{1,17},{2,18},{3,19},{4,20},{5,21},{6,22},{7,23},{8,24},{9,... | collective-permute-start | bytes 98312 | tf_op jit(solution)/shard_map/while/body/eval_jaxpr/ppermute | solution.py:25
  14.1 6.2 collective-permute-start.1
  31.1 7.9 %collective-permute-start.4 = (f32[18,1,130]{2,1,0:T(1,128)}, f32[18,1,130]{2,1,0:T(1,128)}, u32[]{:S(2)}, u32[]{:S(2)}) collective-permute-start(f32[18,1,130]{2,1,0:T(1,128)} %copy.60), channel_id=1, source_target_pairs={{0,1},{1,2},{2,3},{4,5},{5,6},{6,7},{8,9},{9,10},{10,11},{12,13},{... | collective-permute-start | bytes 28088 | tf_op jit(solution)/shard_map/while/body/eval_jaxpr/ppermute | solution.py:25
  36.5 6.0 collective-permute-start.5
  54.1 6.6 %collective-permute-start.1 = (f32[1,64,128]{1,2,0:T(8,128)S(1)}, f32[1,64,128]{1,2,0:T(8,128)S(1)}, u32[]{:S(2)}, u32[]{:S(2)}) collective-permute-start(f32[1,64,128]{1,2,0:T(8,128)S(1)} %get-tuple-element.898), channel_id=1, source_target_pairs={{16,0},{17,1},{18,2},{19,3},{20,4},{21,5},{22,6},{23,7},{24,8},{25... | collective-permute-start | bytes 98312 | tf_op jit(solution)/shard_map/while/body/eval_jaxpr/ppermute | solution.py:27
  72.0 7.4 %collective-permute-start.4 = (f32[18,1,130]{2,1,0:T(1,128)}, f32[18,1,130]{2,1,0:T(1,128)}, u32[]{:S(2)}, u32[]{:S(2)}) collective-permute-start(f32[18,1,130]{2,1,0:T(1,128)} %copy.60), channel_id=1, source_target_pairs={{0,1},{1,2},{2,3},{4,5},{5,6},{6,7},{8,9},{9,10},{10,11},{12,13},{... | collective-permute-start | bytes 28088 | tf_op jit(solution)/shard_map/while/body/eval_jaxpr/ppermute | solution.py:25
  76.8 6.0 collective-permute-start.5
  94.4 6.6 %collective-permute-start.1 = (f32[1,64,128]{1,2,0:T(8,128)S(1)}, f32[1,64,128]{1,2,0:T(8,128)S(1)}, u32[]{:S(2)}, u32[]{:S(2)}) collective-permute-start(f32[1,64,128]{1,2,0:T(8,128)S(1)} %get-tuple-element.898), channel_id=1, source_target_pairs={{16,0},{17,1},{18,2},{19,3},{20,4},{21,5},{22,6},{23,7},{24,8},{25... | collective-permute-start | bytes 98312 | tf_op jit(solution)/shard_map/while/body/eval_jaxpr/ppermute | solution.py:27
  112.3 7.4 %collective-permute-start.4 = (f32[18,1,130]{2,1,0:T(1,128)}, f32[18,1,130]{2,1,0:T(1,128)}, u32[]{:S(2)}, u32[]{:S(2)}) collective-permute-start(f32[18,1,130]{2,1,0:T(1,128)} %copy.60), channel_id=1, source_target_pairs={{0,1},{1,2},{2,3},{4,5},{5,6},{6,7},{8,9},{9,10},{10,11},{12,13},{... | collective-permute-start | bytes 28088 | tf_op jit(solution)/shard_map/while/body/eval_jaxpr/ppermute | solution.py:25
  117.0 6.0 collective-permute-start.5
  134.6 6.6 %collective-permute-start.1 = (f32[1,64,128]{1,2,0:T(8,128)S(1)}, f32[1,64,128]{1,2,0:T(8,128)S(1)}, u32[]{:S(2)}, u32[]{:S(2)}) collective-permute-start(f32[1,64,128]{1,2,0:T(8,128)S(1)} %get-tuple-element.898), channel_id=1, source_target_pairs={{16,0},{17,1},{18,2},{19,3},{20,4},{21,5},{22,6},{23,7},{24,8},{25... | collective-permute-start | bytes 98312 | tf_op jit(solution)/shard_map/while/body/eval_jaxpr/ppermute | solution.py:27
  152.5 6.8 %collective-permute-start.4 = (f32[18,1,130]{2,1,0:T(1,128)}, f32[18,1,130]{2,1,0:T(1,128)}, u32[]{:S(2)}, u32[]{:S(2)}) collective-permute-start(f32[18,1,130]{2,1,0:T(1,128)} %copy.60), channel_id=1, source_target_pairs={{0,1},{1,2},{2,3},{4,5},{5,6},{6,7},{8,9},{9,10},{10,11},{12,13},{... | collective-permute-start | bytes 28088 | tf_op jit(solution)/shard_map/while/body/eval_jaxpr/ppermute | solution.py:25
  156.8 6.0 collective-permute-start.5
  174.0 6.6 %collective-permute-start.18 = (f32[1,64,128]{1,2,0:T(8,128)S(1)}, f32[1,64,128]{1,2,0:T(8,128)S(1)}, u32[]{:S(2)}, u32[]{:S(2)}) collective-permute-start(f32[1,64,128]{1,2,0:T(8,128)S(1)} %get-tuple-element.731), channel_id=1, source_target_pairs={{16,0},{17,1},{18,2},{19,3},{20,4},{21,5},{22,6},{23,7},{24,8},{25... | collective-permute-start | bytes 98312 | tf_op jit(solution)/shard_map/ppermute | solution.py:27
  191.4 52.8 %collective-permute-start.23 = (f32[18,1,130]{2,1,0:T(1,128)}, f32[18,1,130]{2,1,0:T(1,128)}, u32[]{:S(2)}, u32[]{:S(2)}) collective-permute-start(f32[18,1,130]{2,1,0:T(1,128)} %copy.46), channel_id=1, source_target_pairs={{0,1},{1,2},{2,3},{4,5},{5,6},{6,7},{8,9},{9,10},{10,11},{12,13},{... | collective-permute-start | bytes 28088 | tf_op jit(solution)/shard_map/ppermute | solution.py:25
  195.6 50.9 %collective-permute-start.22 = (f32[18,1,130]{2,1,0:T(1,128)}, f32[18,1,130]{2,1,0:T(1,128)}, u32[]{:S(2)}, u32[]{:S(2)}) collective-permute-start(f32[18,1,130]{2,1,0:T(1,128)} %copy.44), channel_id=1, source_target_pairs={{1,0},{2,1},{3,2},{5,4},{6,5},{7,6},{9,8},{10,9},{11,10},{13,12},{... | collective-permute-start | bytes 28088 | tf_op jit(solution)/shard_map/ppermute | solution.py:27
  303.9 5.6 collective-permute-start.7
  316.9 7.0 %collective-permute-start.10 = (f32[10,1,66]{2,1,0:T(1,128)S(1)}, f32[10,1,66]{2,1,0:T(1,128)S(1)}, u32[]{:S(2)}, u32[]{:S(2)}) collective-permute-start(f32[10,1,66]{2,1,0:T(1,128)S(1)} %get-tuple-element.915), channel_id=1, source_target_pairs={{0,1},{1,2},{2,3},{4,5},{5,6},{6,7},{8,9},{9,10},{10,11},{12,13},{... | collective-permute-start | bytes 7928 | tf_op jit(solution)/shard_map/while/body/eval_jaxpr/ppermute | solution.py:25
  321.5 5.5 collective-permute-start.11
  330.3 5.6 collective-permute-start.7
  339.0 5.5 collective-permute-start.9
  346.9 5.5 collective-permute-start.11
  355.8 5.6 collective-permute-start.7
  364.4 5.5 collective-permute-start.9
  370.0 5.8 collective-permute-start.10
  373.4 5.5 collective-permute-start.11
  382.2 5.6 collective-permute-start.7
  390.9 5.5 collective-permute-start.9
  398.4 5.5 collective-permute-start.11
  407.2 5.6 collective-permute-start.24
  413.0 12.5 %collective-permute-start.26 = (f32[10,32,1]{2,1,0:T(8,128)S(1)}, f32[10,32,1]{2,1,0:T(8,128)S(1)}, u32[]{:S(2)}, u32[]{:S(2)}) collective-permute-start(f32[10,32,1]{2,1,0:T(8,128)S(1)} %get-tuple-element.736), channel_id=1, source_target_pairs={{0,4},{4,8},{8,12},{1,5},{5,9},{9,13},{2,6},{6,10},{10,14},{3,7},{... | collective-permute-start | bytes 3848 | tf_op jit(solution)/shard_map/ppermute | solution.py:25
  415.9 9.6 %collective-permute-start.27 = (f32[10,32,1]{2,1,0:T(8,128)S(1)}, f32[10,32,1]{2,1,0:T(8,128)S(1)}, u32[]{:S(2)}, u32[]{:S(2)}) collective-permute-start(f32[10,32,1]{2,1,0:T(8,128)S(1)} %get-tuple-element.735), channel_id=1, source_target_pairs={{4,0},{8,4},{12,8},{5,1},{9,5},{13,9},{6,2},{10,6},{14,10},{7,3},{... | collective-permute-start | bytes 3848 | tf_op jit(solution)/shard_map/ppermute | solution.py:27
  427.9 5.5 collective-permute-start.28
  444.1 5.5 collective-permute-start.13
  451.3 7.2 %collective-permute-start.15 = (f32[6,16,1]{2,1,0:T(8,128)S(1)}, f32[6,16,1]{2,1,0:T(8,128)S(1)}, u32[]{:S(2)}, u32[]{:S(2)}) collective-permute-start(f32[6,16,1]{2,1,0:T(8,128)S(1)} %get-tuple-element.928), channel_id=1, source_target_pairs={{4,0},{8,4},{12,8},{5,1},{9,5},{13,9},{6,2},{10,6},{14,10},{7,3},{... | collective-permute-start | bytes 1160 | tf_op jit(solution)/shard_map/while/body/eval_jaxpr/ppermute | solution.py:27
  460.6 5.5 collective-permute-start.17
  469.2 5.5 collective-permute-start.13
  476.8 5.3 collective-permute-start.15
  484.1 5.5 collective-permute-start.17
  492.7 5.5 collective-permute-start.13
  500.4 5.3 collective-permute-start.15
  507.7 5.5 collective-permute-start.17
  516.3 5.5 collective-permute-start.13
  523.9 5.3 collective-permute-start.15
  531.2 5.5 collective-permute-start.17
  539.8 5.5 collective-permute-start.30
  554.8 5.5 collective-permute-start.34
  574.7 5.4 collective-permute-start.40
  (74 other events, 313.1 us)
where the time goes:
time: 635 us; the launch traced here: 631 us
  local copies, waits for them, and re-layouts  186 us (29%)
  waiting for transfers between devices  176 us (28%)
  starting transfers between devices  162 us (26%)
  other arithmetic  103 us (16%)
    ppermute x45, waiting for transfers between devices, extended_2(): lax.ppermute(head, axis, [((i + 1) % count, i) for i in range(ends)])  156 us
    ppermute x45, starting transfers between devices, extended_2(): lax.ppermute(tail, axis, [(i, (i + 1) % count) for i in range(ends)])  101 us
    reshape x4, local copies, waits for them, and re-layouts, restrict_four(): blocks = field.reshape(first // 2, 2, second // 2, 2, third // 2, 2)  75.6 us
    add x31, other arithmetic, turn(): return (iterate + direction, direction, residual)  64.5 us
    ppermute x45, starting transfers between devices, extended_2(): lax.ppermute(head, axis, [((i + 1) % count, i) for i in range(ends)])  58.3 us
    reduce_sum x6, other arithmetic, restrict_four(): return blocks.sum(axis=(1, 3, 5)) * 0.5  29.8 us
    dynamic_slice x31, local copies, waits for them, and re-layouts, turn(): first_table[turn_index] * direction + second_table[turn_index] * residual  19.1 us
    dynamic_slice x31, local copies, waits for them, and re-layouts, turn(): second_table[turn_index] * residual  18.4 us
  transfers between devices with their start and end apart: 95, of which 58 were waited for; matrix products, arithmetic and copies ran while one was open for 14% of the time, Pallas kernels for 0%

commit v1 on v0

v1 whole, which is shorter than its diff:
```python
import functools

import jax
import jax.numpy as jnp
from jax import lax
from jax.experimental import pallas as pl
from jax.experimental.pallas import tpu as pltpu
from jax.sharding import PartitionSpec as P

DEGREE = 4
LEVELS = 3
BOTTOM_ITERS = 20
LANES = 128

smooth_low = 1.5
smooth_top = 12.0
absorb_top = 1.0
bottom_low = 0.008

MESH = pl.DeviceIdType.MESH
AXES = ("gx", "gz", "gy")


def cheb_tables(count, lower, upper):
    theta = (upper + lower) / 2.0
    delta = (upper - lower) / 2.0
    sigma = theta / delta
    rho_value = 1.0 / sigma
    firsts = []
    seconds = []
    for turn_index in range(count - 1):
        rho_next = 1.0 / (2.0 * sigma - rho_value)
        firsts.append(rho_next * rho_value)
        seconds.append(2.0 * rho_next / delta)
        rho_value = rho_next
    return (1.0 / theta, firsts, seconds)


def exact_dot(left, right):
    return jnp.dot(
        left, right, precision=lax.Precision.HIGHEST, preferred_element_type=jnp.float32
    )


def lanes_of(shape):
    return lax.broadcasted_iota(jnp.int32, shape, len(shape) - 1)


def rows_of(shape):
    return lax.broadcasted_iota(jnp.int32, shape, len(shape) - 2)


def halving():
    j = rows_of((LANES, LANES))
    i = lanes_of((LANES, LANES))
    return jnp.where(j // 2 == i, jnp.float32(0.5), jnp.float32(0.0))


def trilinear(coarse, fine):
    centre = fine // 2
    other = centre + 2 * (fine % 2) - 1
    return jnp.where(coarse == centre, jnp.float32(0.75), jnp.float32(0.0)) + jnp.where(
        coarse == other, jnp.float32(0.25), jnp.float32(0.0)
    )


def kernel(sizes, blocks, tab, rs, ab, out0, out1, out2, *scratch):
    nx, nz, ny = sizes
    me = {a: lax.axis_index(a) for a in AXES}
    count = dict(zip(AXES, sizes))
    has_lo = {a: me[a] > 0 for a in AXES}
    has_hi = {a: me[a] < count[a] - 1 for a in AXES}

    per_level = 9
    level_refs = [scratch[per_level * k : per_level * (k + 1)] for k in range(LEVELS)]
    rest = scratch[per_level * LEVELS :]
    pairs, gath, src3, coef3, dir3, res3, it3, send_sem, recv_sem, gsend, grecv = rest

    barrier = pltpu.get_barrier_semaphore()
    greeted = 0
    for a in AXES:
        for k in range(1, count[a]):
            pl.semaphore_signal(
                barrier,
                inc=1,
                device_id={a: lax.rem(me[a] + k, count[a])},
                device_id_type=MESH,
            )
            greeted += 1
    pl.semaphore_wait(barrier, greeted)

    half = halving()

    def restrict(read, shape):
        first, second, _ = shape
        for x in range(first // 2):
            pairs[pl.ds(x * second, second), :] = read(2 * x) + read(2 * x + 1)
        total = first // 2 * second // 2
        summed = (
            pairs[pl.ds(0, total, stride=2), :] + pairs[pl.ds(1, total, stride=2), :]
        )
        return exact_dot(summed, half)

    def copies(level, r):
        first, second, _ = blocks[level]
        dirs, faces_z, faces_y, halo_x, halo_z, halo_y = level_refs[level][:6]
        slot = level * (DEGREE + 1) + r
        ends = {
            "gx": (dirs.at[r, 1], dirs.at[r, first], halo_x),
            "gz": (faces_z.at[r, 0], faces_z.at[r, 1], halo_z),
            "gy": (faces_y.at[r], faces_y.at[r], halo_y),
        }
        made = []
        for n, a in enumerate(AXES):
            low_face, high_face, halo = ends[a]
            made.append(
                (
                    has_lo[a],
                    has_hi[a],
                    pltpu.make_async_remote_copy(
                        src_ref=low_face,
                        dst_ref=halo.at[r, 1],
                        send_sem=send_sem.at[slot, 2 * n],
                        recv_sem=recv_sem.at[slot, 2 * n],
                        device_id={a: jnp.maximum(me[a] - 1, 0)},
                        device_id_type=MESH,
                    ),
                )
            )
            made.append(
                (
                    has_hi[a],
                    has_lo[a],
                    pltpu.make_async_remote_copy(
                        src_ref=high_face,
                        dst_ref=halo.at[r, 0],
                        send_sem=send_sem.at[slot, 2 * n + 1],
                        recv_sem=recv_sem.at[slot, 2 * n + 1],
                        device_id={a: jnp.minimum(me[a] + 1, count[a] - 1)},
                        device_id_type=MESH,
                    ),
                )
            )
        return made

    def start(level, r):
        for sends, _, copy in copies(level, r):
            pl.when(sends)(copy.start)

    def arrive(level, r):
        for _, gets, copy in copies(level, r):
            pl.when(gets)(copy.wait_recv)

    def sent(level, r):
        for sends, _, copy in copies(level, r):
            pl.when(sends)(copy.wait_send)

    def put_faces(level, r, x, field, packed):
        second, width = blocks[level][1:]
        dirs, faces_z = level_refs[level][:2]
        dirs[r, x + 1] = field
        faces_z[r, 0, pl.ds(x, 1), :] = field[:1]
        faces_z[r, 1, pl.ds(x, 1), :] = field[second - 1 :]
        lane = lanes_of((second, LANES))
        low = pltpu.roll(field, 2 * x + 1, 1)
        if width == LANES:
            return jnp.where(lane // 2 == x, low, packed)
        high = pltpu.roll(field, 2 * x + LANES + 1 - width, 1)
        return jnp.where(lane == 2 * x + 1, low, jnp.where(lane == 2 * x, high, packed))

    def inside(level, r, base, coef):
        first, second, width = blocks[level]
        dirs = level_refs[level][0]
        resid = level_refs[level][6]
        row = rows_of((second, LANES))
        lane = lanes_of((second, LANES))

        @pl.loop(0, first)
        def _(x):
            d = dirs[r, x + 1]
            near = dirs[r, x] + dirs[r, x + 2]
            near += jnp.where(row == 0, 0.0, pltpu.roll(d, 1, 0))
            near += jnp.where(row == second - 1, 0.0, pltpu.roll(d, second - 1, 0))
            near += pltpu.roll(d, 1, 1) + pltpu.roll(d, LANES - 1, 1)
            if width < LANES:
                near = jnp.where(lane < width, near, 0.0)
            resid[x] = base[x] - ((6.0 + coef[x]) * d - near)

    def outside(level, r):
        first, second, width = blocks[level]
        faces_y, halo_x, halo_z, halo_y = level_refs[level][2:6]
        resid = level_refs[level][6]
        row = rows_of((second, LANES))
        lane = lanes_of((second, LANES))
        resid[0] += jnp.where(has_lo["gx"], halo_x[r, 0], 0.0)
        resid[first - 1] += jnp.where(has_hi["gx"], halo_x[r, 1], 0.0)
        low = jnp.where(has_lo["gy"], halo_y[r, 0], 0.0)
        high = jnp.where(has_hi["gy"], halo_y[r, 1], 0.0)
        if width == LANES:
            low -= faces_y[r]
            high -= faces_y[r]
        ends = jnp.where(lane % 2 == 1, pltpu.roll(low, 1, 1), pltpu.roll(high, LANES - 1, 1))

        def add(x):
            res = resid[x]
            z_low = jnp.where(has_lo["gz"], halo_z[r, 0, pl.ds(x, 1), :], 0.0)
            z_high = jnp.where(has_hi["gz"], halo_z[r, 1, pl.ds(x, 1), :], 0.0)
            res += jnp.where(row == 0, z_low, 0.0) + jnp.where(row == second - 1, z_high, 0.0)
            to_low = pltpu.roll(ends, LANES - 1 - 2 * x, 1)
            if width == LANES:
                res += jnp.where((lane == 0) | (lane == LANES - 1), to_low, 0.0)
            else:
                to_high = pltpu.roll(ends, width - 1 - 2 * x, 1)
                res += jnp.where(lane == 0, to_low, jnp.where(lane == width - 1, to_high, 0.0))
            return res

        return add

    def pack_zero(level):
        return jnp.zeros((blocks[level][1], LANES), jnp.float32)

    def smooth(level, source, coef, between):
        first, second, width = blocks[level]
        dirs, _, faces_y = level_refs[level][:3]
        resid, iterate = level_refs[level][6:8]
        upper = smooth_top + 4.0**level * absorb_top
        scale, firsts, seconds = cheb_tables(DEGREE + 1, smooth_low, upper)
        empty = jnp.zeros((second, LANES), jnp.float32)
        for r in range(DEGREE + 1):
            dirs[r, 0] = empty
            dirs[r, first + 1] = empty

        def opening(x, packed):
            d = source[x] * scale
            iterate[x] = d
            return put_faces(level, 0, x, d, packed)

        faces_y[0] = lax.fori_loop(0, first, opening, empty)
        for r in range(DEGREE + 1):
            start(level, r)
            inside(level, r, source if r in (0, DEGREE) else resid, coef)
            if r == 0:
                between()
            arrive(level, r)
            add = outside(level, r)
            if r == DEGREE:

                @pl.loop(0, first)
                def _(x):
                    resid[x] = add(x)

            else:

                def turn(x, packed, r=r, add=add):
                    res = add(x)
                    resid[x] = res
                    d = firsts[r] * dirs[r, x + 1] + seconds[r] * res
                    total = iterate[x] + d
                    iterate[x] = total
                    return put_faces(level, r + 1, x, total if r == DEGREE - 1 else d, packed)

                faces_y[r + 1] = lax.fori_loop(0, first, turn, empty)

    bottom = tuple(s // 2 for s in blocks[-1])
    coefs = [ab] + [level_refs[k][8] for k in range(1, LEVELS)]
    sources = [rs] + [level_refs[k][8] for k in range(1, LEVELS)]
    coefs = [ab, level_refs[1][8].at[0], level_refs[2][8].at[0]]
    sources = [rs, level_refs[1][8].at[1], level_refs[2][8].at[1]]
    message = gath.at[me["gx"], me["gy"], me["gz"]]

    def spread(rows, shape, ref):
        for x in range(shape[0]):
            ref[x] = rows[x * shape[1] : (x + 1) * shape[1]]

    def into_message(rows, first_part):
        packed = jnp.zeros((bottom[1], LANES), jnp.float32)
        for x in range(bottom[0]):
            part = rows[x * bottom[1] : (x + 1) * bottom[1]]
            shift = (first_part + x) * bottom[2]
            packed += pltpu.roll(part, shift, 1) if shift else part
        return packed

    def coarsen():
        for level in range(1, LEVELS):
            rows = restrict(lambda x: coefs[level - 1][x], blocks[level - 1])
            spread(rows, blocks[level], coefs[level])
        rows = restrict(lambda x: coefs[LEVELS - 1][x], blocks[LEVELS - 1])
        message[...] = into_message(rows, bottom[0])

    for level in range(LEVELS):
        smooth(level, sources[level], coefs[level], coarsen if level == 0 else lambda: None)
        resid = level_refs[level][6]
        rows = restrict(lambda x: resid[x], blocks[level])
        if level + 1 < LEVELS:
            spread(rows, blocks[level + 1], sources[level + 1])
    message[...] += into_message(rows, 0)

    pieces = {
        "gz": message,
        "gx": gath.at[me["gx"], me["gy"]],
        "gy": gath.at[:, me["gy"]],
    }
    base = 0
    for a in ("gz", "gx", "gy"):
        made = []
        for k in range(1, count[a]):
            made.append(
                pltpu.make_async_remote_copy(
                    src_ref=pieces[a],
                    dst_ref=pieces[a],
                    send_sem=gsend.at[base],
                    recv_sem=grecv.at[base],
                    device_id={a: lax.rem(me[a] + k, count[a])},
                    device_id_type=MESH,
                )
            )
            base += 1
        for copy in made:
            copy.start()
        for copy in made:
            copy.wait_recv()
        for copy in made:
            copy.wait_send()

    bx, bz, by = bottom
    whole_x, whole_z, whole_y = bx * nx, bz * nz, by * ny
    lane = lanes_of((bz, LANES))

    def place(n, carry):
        ix = n // nz
        iz = n % nz
        for part, ref in ((0, src3), (bx, coef3)):
            for x in range(bx):
                tile = jnp.zeros((bz, LANES), jnp.float32)
                for iy in range(ny):
                    shift = (iy - part - x) * by % LANES
                    moved = gath[ix, iy, iz]
                    if shift:
                        moved = pltpu.roll(moved, shift, 1)
                    tile = jnp.where(lane // by == iy, moved, tile)
                ref[ix * bx + x, pl.ds(pl.multiple_of(iz * bz, bz), bz), :] = tile
        return carry

    lax.fori_loop(0, nx * nz, place, 0)

    upper = smooth_top + 4.0**LEVELS * absorb_top
    scale = cheb_tables(BOTTOM_ITERS, bottom_low, upper)[0]
    zero = jnp.zeros((whole_z, LANES), jnp.float32)
    row = rows_of((whole_z, LANES))
    lane = lanes_of((whole_z, LANES))
    for ref in (dir3, it3):
        ref[0] = zero
        ref[whole_x + 1] = zero
    for x in range(whole_x):
        source = src3[x]
        res3[x] = source
        dir3[x + 1] = source * scale
        it3[x + 1] = source * scale

    def bottom_turn(n, carry):
        one = tab[0, n]
        two = tab[1, n]
        layers = [dir3[x] for x in range(whole_x + 2)]
        for x in range(whole_x):
            d = layers[x + 1]
            near = layers[x] + layers[x + 2]
            near += jnp.where(row == 0, 0.0, pltpu.roll(d, 1, 0))
            near += jnp.where(row == whole_z - 1, 0.0, pltpu.roll(d, whole_z - 1, 0))
            if whole_y < LANES:
                near += pltpu.roll(d, 1, 1) + pltpu.roll(d, LANES - 1, 1)
                near = jnp.where(lane < whole_y, near, 0.0)
            else:
                near += jnp.where(lane == 0, 0.0, pltpu.roll(d, 1, 1))
                near += jnp.where(lane == LANES - 1, 0.0, pltpu.roll(d, LANES - 1, 1))
            res = res3[x] - ((6.0 + coef3[x]) * d - near)
            res3[x] = res
            d = one * d + two * res
            dir3[x + 1] = d
            it3[x + 1] += d
        return carry

    lax.fori_loop(0, BOTTOM_ITERS - 1, bottom_turn, 0)

    first, second, width = blocks[-1]
    i = lanes_of((LANES, LANES))
    along_y = jnp.where(
        i < width, trilinear(rows_of((LANES, LANES)), me["gy"] * width + i), 0.0
    )
    along_z = trilinear(
        lanes_of((second, whole_z)), me["gz"] * second + rows_of((second, whole_z))
    )
    layers = []
    for x in range(first):
        centre = me["gx"] * (first // 2) + x // 2 + 1
        layers.append(0.75 * it3[centre] + 0.25 * it3[centre + 2 * (x % 2) - 1])
    moved = exact_dot(jnp.concatenate(layers, axis=0), along_y)
    iterate = level_refs[-1][7]
    for x in range(first):
        fine = exact_dot(along_z, moved[x * whole_z : (x + 1) * whole_z])
        out2[x] = (iterate[x] + fine)[:, :width]

    first, second, width = blocks[0]

    @pl.loop(0, first)
    def _(x):
        out0[x] = level_refs[0][7][x]

    first, second, width = blocks[1]
    for x in range(first):
        out1[x] = level_refs[1][7][x][:, :width]

    for level in range(LEVELS):
        for r in range(DEGREE + 1):
            sent(level, r)


def on_device(sizes, right_side, absorption):
    nx, nz, ny = sizes
    blocks = [tuple(s // 2**k for s in right_side.shape) for k in range(LEVELS)]
    rounds = DEGREE + 1
    scratch = []
    for first, second, width in blocks:
        scratch += [
            pltpu.VMEM((rounds, first + 2, second, LANES), jnp.float32),
            pltpu.VMEM((rounds, 2, first, LANES), jnp.float32),
            pltpu.VMEM((rounds, second, LANES), jnp.float32),
            pltpu.VMEM((rounds, 2, second, LANES), jnp.float32),
            pltpu.VMEM((rounds, 2, first, LANES), jnp.float32),
            pltpu.VMEM((rounds, 2, second, LANES), jnp.float32),
            pltpu.VMEM((first, second, LANES), jnp.float32),
            pltpu.VMEM((first, second, LANES), jnp.float32),
            pltpu.VMEM((2, first, second, LANES), jnp.float32),
        ]
    bx, bz, by = (s // 2 for s in blocks[-1])
    whole = (bx * nx, bz * nz, LANES)
    padded = (bx * nx + 2, bz * nz, LANES)
    lines = nx + ny + nz - 3
    scratch += [
        pltpu.VMEM((blocks[0][0] // 2 * blocks[0][1], LANES), jnp.float32),
        pltpu.VMEM((nx, ny, nz, bz, LANES), jnp.float32),
        pltpu.VMEM(whole, jnp.float32),
        pltpu.VMEM(whole, jnp.float32),
        pltpu.VMEM(padded, jnp.float32),
        pltpu.VMEM(whole, jnp.float32),
        pltpu.VMEM(padded, jnp.float32),
        pltpu.SemaphoreType.DMA((LEVELS * rounds, 6)),
        pltpu.SemaphoreType.DMA((LEVELS * rounds, 6)),
        pltpu.SemaphoreType.DMA((lines,)),
        pltpu.SemaphoreType.DMA((lines,)),
    ]
    upper = smooth_top + 4.0**LEVELS * absorb_top
    _, firsts, seconds = cheb_tables(BOTTOM_ITERS, bottom_low, upper)
    table = jnp.asarray([firsts, seconds], jnp.float32)
    vmem = pl.BlockSpec(memory_space=pltpu.VMEM)
    return pl.pallas_call(
        functools.partial(kernel, sizes, blocks),
        out_shape=tuple(jax.ShapeDtypeStruct(b, jnp.float32) for b in blocks),
        in_specs=[pl.BlockSpec(memory_space=pltpu.SMEM), vmem, vmem],
        out_specs=(vmem, vmem, vmem),
        scratch_shapes=scratch,
        compiler_params=pltpu.CompilerParams(
            collective_id=0, has_side_effects=True, vmem_limit_bytes=48 * 1024 * 1024
        ),
    )(table, right_side, absorption)


def solution(mesh):
    sizes = tuple(mesh.shape[a] for a in AXES)
    spec = P("gx", "gz", "gy")
    return jax.shard_map(
        functools.partial(on_device, sizes),
        mesh=mesh,
        in_specs=(spec, spec),
        out_specs=(spec, spec, spec),
        check_vma=False,
    )
```

time: 635 us -> 91 us (0.14)
  local copies, waits for them, and re-layouts: 186 us -> 4.82 us
  waiting for transfers between devices: 176 us -> 0 us
  starting transfers between devices: 162 us -> 0 us
  other arithmetic: 103 us -> 0 us
  Pallas kernels: 0 us -> 85.3 us
    ppermute x95 -> x0, waiting for transfers between devices: 176 us -> none  [the longest x45 156 us: extended_2(): lax.ppermute(head, axis, [((i + 1) % count, i) for i in range(ends)])]
    ppermute x95 -> x0, starting transfers between devices: 162 us -> none  [the longest x45 101 us: extended_2(): lax.ppermute(tail, axis, [(i, (i + 1) % count) for i in range(ends)])]
    pallas_call x0 -> x1, Pallas kernels: none -> 85.3 us  [on_device(): pl.pallas_call(functools.partial(kernel, sizes, blocks), out_shape=tuple(...]
    reshape x4 -> x0, local copies, waits for them, and re-layouts: 75.6 us -> none  [restrict_four(): blocks = field.reshape(first // 2, 2, second // 2, 2, third // 2, 2)]
    add x32 -> x0, other arithmetic: 64.5 us -> none  [the longest x31 64.5 us: turn(): return (iterate + direction, direction, residual)]
    dynamic_slice x62 -> x0, local copies, waits for them, and re-layouts: 37.5 us -> none  [the longest x31 19.1 us: turn(): first_table[turn_index] * direction + second_table[turn_index] * residual]
    reduce_sum x6 -> x0, other arithmetic: 29.8 us -> none  [restrict_four(): return blocks.sum(axis=(1, 3, 5)) * 0.5]
    slice x45 -> x0, local copies, waits for them, and re-layouts: 28.5 us -> none  [the longest x40 15.6 us: extended_2(): head = lax.slice_in_dim(cells, 0, width, axis=dim)]
  transfers between devices with their start and end apart: 95 -> 0, of which waited for: 58 -> 0; matrix products, arithmetic and copies ran while one was open for 14% -> 0% of each run, Pallas kernels for 0% -> 0%
where the time goes in v1:
time: 91 us; the launch traced here: 90.8 us
  Pallas kernels  85.3 us (94%)
  local copies, waits for them, and re-layouts  4.82 us (5%)
    pallas_call x1, Pallas kernels, on_device(): pl.pallas_call(functools.partial(kernel, sizes, blocks), out_shape=tuple(...  85.3 us
    unnamed x9, local copies, waits for them, and re-layouts  4.82 us

profile of v1, /device:TPU:0, one launch (start us, length us, event | category | flops | bytes accessed | tf_op | source)
XLA Modules:
  0.0 90.8 jit_solution(5670467032519994368)
XLA Ops:
  0.6 0.0 copy-start
  0.6 1.0 %copy-done = f32[16,64,128]{2,1,0:T(8,128)S(1)} copy-done((f32[16,64,128]{2,1,0:T(8,128)S(1)}, f32[16,64,128]{2,1,0:T(8,128)}, u32[]{:S(2)}) %copy-start) | copy-done | bytes 524312
  1.7 0.0 copy-start.1
  1.7 1.0 %copy-done.1 = f32[16,64,128]{2,1,0:T(8,128)S(1)} copy-done((f32[16,64,128]{2,1,0:T(8,128)S(1)}, f32[16,64,128]{2,1,0:T(8,128)}, u32[]{:S(2)}) %copy-start.1) | copy-done | bytes 524312
  2.7 0.0 copy-start.2
  2.7 0.7 copy-done.2
  3.4 85.3 %shard_map.58 = (f32[16,64,128]{2,1,0:T(8,128)S(1)}, f32[8,32,64]{2,1,0:T(8,128)S(1)}, f32[4,16,32]{2,1,0:T(8,128)S(1)}) custom-call(f32[2,19]{1,0:T(2,128)S(1)} %copy-done.2, f32[16,64,128]{2,1,0:T(8,128)S(1)} %copy-done, f32[16,64,128]{2,1,0:T(8,128)S(1)} %copy-done.1), custom_call_target="tpu_custom_call" | custom-call | tf_op jit(solution)/shard_map/pallas_call | solution.py:455
  88.7 0.8 copy.9
  89.5 0.7 copy.10
  90.2 0.6 copy.11
Async XLA Ops:
  0.6 1.0 %copy-start = (f32[16,64,128]{2,1,0:T(8,128)S(1)}, f32[16,64,128]{2,1,0:T(8,128)}, u32[]{:S(2)}) copy-start(f32[16,64,128]{2,1,0:T(8,128)} %rs.1) | copy-start | bytes 1572868
  1.7 1.0 %copy-start.1 = (f32[16,64,128]{2,1,0:T(8,128)S(1)}, f32[16,64,128]{2,1,0:T(8,128)}, u32[]{:S(2)}) copy-start(f32[16,64,128]{2,1,0:T(8,128)} %ab.1) | copy-start | bytes 1572868
  2.7 0.7 copy-start.2

commit v2 on v1

--- a/solution.py
+++ b/solution.py
@@ -72,7 +72,8 @@
     has_hi = {a: me[a] < count[a] - 1 for a in AXES}
 
     per_level = 9
-    level_refs = [scratch[per_level * k : per_level * (k + 1)] for k in range(LEVELS)]
+    level_refs = [list(scratch[per_level * k : per_level * (k + 1)]) for k in range(LEVELS)]
+    level_refs[0][7] = out0
     rest = scratch[per_level * LEVELS :]
     pairs, gath, src3, coef3, dir3, res3, it3, send_sem, recv_sem, gsend, grecv = rest
 
@@ -168,29 +169,54 @@
         high = pltpu.roll(field, 2 * x + LANES + 1 - width, 1)
         return jnp.where(lane == 2 * x + 1, low, jnp.where(lane == 2 * x, high, packed))
 
+    def by_chunks(level, body, carry):
+        first, second, _ = blocks[level]
+        chunk = min(first, 256 // second)
+
+        def turn(n, carry):
+            return body([n * chunk + j for j in range(chunk)], carry)
+
+        if chunk == first:
+            return turn(0, carry)
+        return lax.fori_loop(0, first // chunk, turn, carry)
+
+    edge_row = rows_of((8, LANES))
+
     def inside(level, r, base, coef):
         first, second, width = blocks[level]
         dirs = level_refs[level][0]
         resid = level_refs[level][6]
-        row = rows_of((second, LANES))
         lane = lanes_of((second, LANES))
 
-        @pl.loop(0, first)
-        def _(x):
-            d = dirs[r, x + 1]
-            near = dirs[r, x] + dirs[r, x + 2]
-            near += jnp.where(row == 0, 0.0, pltpu.roll(d, 1, 0))
-            near += jnp.where(row == second - 1, 0.0, pltpu.roll(d, second - 1, 0))
-            near += pltpu.roll(d, 1, 1) + pltpu.roll(d, LANES - 1, 1)
-            if width < LANES:
-                near = jnp.where(lane < width, near, 0.0)
-            resid[x] = base[x] - ((6.0 + coef[x]) * d - near)
+        def body(xs, carry):
+            layers = [dirs[r, xs[0] + j] for j in range(len(xs) + 2)]
+            bases = [base[x] for x in xs]
+            parts = [coef[x] for x in xs]
+            results = []
+            for j in range(len(xs)):
+                d = layers[j + 1]
+                near = layers[j] + layers[j + 2]
+                up = pltpu.roll(d, 1, 0)
+                down = pltpu.roll(d, second - 1, 0)
+                up = jnp.concatenate((jnp.where(edge_row == 0, 0.0, up[:8]), up[8:]), 0)
+                down = jnp.concatenate(
+                    (down[: second - 8], jnp.where(edge_row == 7, 0.0, down[second - 8 :])), 0
+                )
+                near += up + down
+                near += pltpu.roll(d, 1, 1) + pltpu.roll(d, LANES - 1, 1)
+                if width < LANES:
+                    near = jnp.where(lane < width, near, 0.0)
+                results.append(bases[j] - ((6.0 + parts[j]) * d - near))
+            for j, x in enumerate(xs):
+                resid[x] = results[j]
+            return carry
+
+        by_chunks(level, body, 0)
 
     def outside(level, r):
         first, second, width = blocks[level]
         faces_y, halo_x, halo_z, halo_y = level_refs[level][2:6]
         resid = level_refs[level][6]
-        row = rows_of((second, LANES))
         lane = lanes_of((second, LANES))
         resid[0] += jnp.where(has_lo["gx"], halo_x[r, 0], 0.0)
         resid[first - 1] += jnp.where(has_hi["gx"], halo_x[r, 1], 0.0)
@@ -205,7 +231,14 @@
             res = resid[x]
             z_low = jnp.where(has_lo["gz"], halo_z[r, 0, pl.ds(x, 1), :], 0.0)
             z_high = jnp.where(has_hi["gz"], halo_z[r, 1, pl.ds(x, 1), :], 0.0)
-            res += jnp.where(row == 0, z_low, 0.0) + jnp.where(row == second - 1, z_high, 0.0)
+            res = jnp.concatenate(
+                (
+                    res[:8] + jnp.where(edge_row == 0, z_low, 0.0),
+                    res[8 : second - 8],
+                    res[second - 8 :] + jnp.where(edge_row == 7, z_high, 0.0),
+                )[:: 1 if second > 16 else 2],
+                0,
+            )
             to_low = pltpu.roll(ends, LANES - 1 - 2 * x, 1)
             if width == LANES:
                 res += jnp.where((lane == 0) | (lane == LANES - 1), to_low, 0.0)
@@ -215,9 +248,6 @@
             return res
 
         return add
-
-    def pack_zero(level):
-        return jnp.zeros((blocks[level][1], LANES), jnp.float32)
 
     def smooth(level, source, coef, between):
         first, second, width = blocks[level]
@@ -230,12 +260,14 @@
             dirs[r, 0] = empty
             dirs[r, first + 1] = empty
 
-        def opening(x, packed):
-            d = source[x] * scale
-            iterate[x] = d
-            return put_faces(level, 0, x, d, packed)
-
-        faces_y[0] = lax.fori_loop(0, first, opening, empty)
+        def opening(xs, packed):
+            fields = [source[x] * scale for x in xs]
+            for x, d in zip(xs, fields):
+                iterate[x] = d
+                packed = put_faces(level, 0, x, d, packed)
+            return packed
+
+        faces_y[0] = by_chunks(level, opening, empty)
         for r in range(DEGREE + 1):
             start(level, r)
             inside(level, r, source if r in (0, DEGREE) else resid, coef)
@@ -243,27 +275,33 @@
                 between()
             arrive(level, r)
             add = outside(level, r)
+
+            def last(xs, carry, add=add):
+                results = [add(x) for x in xs]
+                for x, res in zip(xs, results):
+                    resid[x] = res
+                return carry
+
+            def turn(xs, packed, r=r, add=add):
+                results = [add(x) for x in xs]
+                fields = [
+                    firsts[r] * dirs[r, x + 1] + seconds[r] * res for x, res in zip(xs, results)
+                ]
+                totals = [iterate[x] + d for x, d in zip(xs, fields)]
+                for x, res, d, total in zip(xs, results, fields, totals):
+                    resid[x] = res
+                    iterate[x] = total
+                    packed = put_faces(
+                        level, r + 1, x, total if r == DEGREE - 1 else d, packed
+                    )
+                return packed
+
             if r == DEGREE:
-
-                @pl.loop(0, first)
-                def _(x):
-                    resid[x] = add(x)
-
+                by_chunks(level, last, 0)
             else:
-
-                def turn(x, packed, r=r, add=add):
-                    res = add(x)
-                    resid[x] = res
-                    d = firsts[r] * dirs[r, x + 1] + seconds[r] * res
-                    total = iterate[x] + d
-                    iterate[x] = total
-                    return put_faces(level, r + 1, x, total if r == DEGREE - 1 else d, packed)
-
-                faces_y[r + 1] = lax.fori_loop(0, first, turn, empty)
+                faces_y[r + 1] = by_chunks(level, turn, empty)
 
     bottom = tuple(s // 2 for s in blocks[-1])
-    coefs = [ab] + [level_refs[k][8] for k in range(1, LEVELS)]
-    sources = [rs] + [level_refs[k][8] for k in range(1, LEVELS)]
     coefs = [ab, level_refs[1][8].at[0], level_refs[2][8].at[0]]
     sources = [rs, level_refs[1][8].at[1], level_refs[2][8].at[1]]
     message = gath.at[me["gx"], me["gy"], me["gz"]]
@@ -398,12 +436,6 @@
     for x in range(first):
         fine = exact_dot(along_z, moved[x * whole_z : (x + 1) * whole_z])
         out2[x] = (iterate[x] + fine)[:, :width]
-
-    first, second, width = blocks[0]
-
-    @pl.loop(0, first)
-    def _(x):
-        out0[x] = level_refs[0][7][x]
 
     first, second, width = blocks[1]
     for x in range(first):

time: 91 us -> 75.4 us (0.83)
  Pallas kernels: 85.3 us -> 69.7 us
    pallas_call x1, Pallas kernels: 85.3 us -> 69.7 us  [on_device(): pl.pallas_call(functools.partial(kernel, sizes, blocks), out_shape=tuple(...]
where the time goes in v2:
time: 75.4 us; the launch traced here: 75.2 us
  Pallas kernels  69.7 us (92%)
  local copies, waits for them, and re-layouts  4.82 us (6%)
    pallas_call x1, Pallas kernels, on_device(): pl.pallas_call(functools.partial(kernel, sizes, blocks), out_shape=tuple(...  69.7 us
    unnamed x9, local copies, waits for them, and re-layouts  4.82 us

profile of v2, /device:TPU:0, one launch (start us, length us, event | category | flops | bytes accessed | tf_op | source)
XLA Modules:
  0.0 75.2 jit_solution(16676505724987815499)
XLA Ops:
  0.6 0.0 copy-start
  0.6 1.0 %copy-done = f32[16,64,128]{2,1,0:T(8,128)S(1)} copy-done((f32[16,64,128]{2,1,0:T(8,128)S(1)}, f32[16,64,128]{2,1,0:T(8,128)}, u32[]{:S(2)}) %copy-start) | copy-done | bytes 524312
  1.7 0.0 copy-start.1
  1.7 1.0 %copy-done.1 = f32[16,64,128]{2,1,0:T(8,128)S(1)} copy-done((f32[16,64,128]{2,1,0:T(8,128)S(1)}, f32[16,64,128]{2,1,0:T(8,128)}, u32[]{:S(2)}) %copy-start.1) | copy-done | bytes 524312
  2.7 0.0 copy-start.2
  2.7 0.7 copy-done.2
  3.4 69.7 %shard_map.58 = (f32[16,64,128]{2,1,0:T(8,128)S(1)}, f32[8,32,64]{2,1,0:T(8,128)S(1)}, f32[4,16,32]{2,1,0:T(8,128)S(1)}) custom-call(f32[2,19]{1,0:T(2,128)S(1)} %copy-done.2, f32[16,64,128]{2,1,0:T(8,128)S(1)} %copy-done, f32[16,64,128]{2,1,0:T(8,128)S(1)} %copy-done.1), custom_call_target="tpu_custom_call" | custom-call | tf_op jit(solution)/shard_map/pallas_call | solution.py:487
  73.1 0.8 %copy.9 = f32[16,64,128]{2,1,0:T(8,128)} copy(f32[16,64,128]{2,1,0:T(8,128)S(1)} %get-tuple-element.6) | data formatting | bytes 1048576
  73.9 0.7 copy.10
  74.5 0.6 copy.11
Async XLA Ops:
  0.6 1.0 %copy-start = (f32[16,64,128]{2,1,0:T(8,128)S(1)}, f32[16,64,128]{2,1,0:T(8,128)}, u32[]{:S(2)}) copy-start(f32[16,64,128]{2,1,0:T(8,128)} %rs.1) | copy-start | bytes 1572868
  1.7 1.0 %copy-start.1 = (f32[16,64,128]{2,1,0:T(8,128)S(1)}, f32[16,64,128]{2,1,0:T(8,128)}, u32[]{:S(2)}) copy-start(f32[16,64,128]{2,1,0:T(8,128)} %ab.1) | copy-start | bytes 1572868
  2.7 0.7 copy-start.2

commit v3 on v2

--- a/solution.py
+++ b/solution.py
@@ -9,6 +9,7 @@
 
 DEGREE = 4
 LEVELS = 3
+SPLIT = 2
 BOTTOM_ITERS = 20
 LANES = 128
 
@@ -64,7 +65,7 @@
     )
 
 
-def kernel(sizes, blocks, tab, rs, ab, out0, out1, out2, *scratch):
+def kernel(sizes, blocks, rs_hbm, ab_hbm, out0, out1, out2, *scratch):
     nx, nz, ny = sizes
     me = {a: lax.axis_index(a) for a in AXES}
     count = dict(zip(AXES, sizes))
@@ -72,10 +73,26 @@
     has_hi = {a: me[a] < count[a] - 1 for a in AXES}
 
     per_level = 9
-    level_refs = [list(scratch[per_level * k : per_level * (k + 1)]) for k in range(LEVELS)]
+    level_refs = [list(scratch[per_level * k : per_level * (k + 1)]) for k in range(SPLIT)]
     level_refs[0][7] = out0
-    rest = scratch[per_level * LEVELS :]
-    pairs, gath, src3, coef3, dir3, res3, it3, send_sem, recv_sem, gsend, grecv = rest
+    rest = scratch[per_level * SPLIT :]
+    rs, ab, pairs, gath_s, gath_c, src2, coef2, dir2, res2, it2 = rest[:10]
+    src3, coef3, dir3, res3, it3, tab = rest[10:16]
+    send_sem, recv_sem, gsend, grecv, fetch_sem = rest[16:]
+
+    fetches = [
+        pltpu.make_async_copy(rs_hbm, rs, fetch_sem.at[0]),
+        pltpu.make_async_copy(ab_hbm, ab, fetch_sem.at[1]),
+    ]
+    for fetch in fetches:
+        fetch.start()
+
+    bottom_scale, firsts, seconds = cheb_tables(
+        BOTTOM_ITERS, bottom_low, smooth_top + 4.0**LEVELS * absorb_top
+    )
+    for n in range(BOTTOM_ITERS - 1):
+        tab[0, n] = jnp.float32(firsts[n])
+        tab[1, n] = jnp.float32(seconds[n])
 
     barrier = pltpu.get_barrier_semaphore()
     greeted = 0
@@ -270,9 +287,11 @@
         faces_y[0] = by_chunks(level, opening, empty)
         for r in range(DEGREE + 1):
             start(level, r)
+            if level == 0 and r == 0:
+                fetches[1].wait()
             inside(level, r, source if r in (0, DEGREE) else resid, coef)
-            if r == 0:
-                between()
+            if r in between:
+                between[r]()
             arrive(level, r)
             add = outside(level, r)
 
@@ -301,147 +320,214 @@
             else:
                 faces_y[r + 1] = by_chunks(level, turn, empty)
 
-    bottom = tuple(s // 2 for s in blocks[-1])
-    coefs = [ab, level_refs[1][8].at[0], level_refs[2][8].at[0]]
-    sources = [rs, level_refs[1][8].at[1], level_refs[2][8].at[1]]
-    message = gath.at[me["gx"], me["gy"], me["gz"]]
+    coef1, source1 = level_refs[1][8].at[0], level_refs[1][8].at[1]
+    first2, second2, width2 = blocks[2]
+    whole2 = (first2 * nx, second2 * nz, width2 * ny)
+    whole3 = tuple(s // 2 for s in whole2)
 
     def spread(rows, shape, ref):
         for x in range(shape[0]):
             ref[x] = rows[x * shape[1] : (x + 1) * shape[1]]
 
-    def into_message(rows, first_part):
-        packed = jnp.zeros((bottom[1], LANES), jnp.float32)
-        for x in range(bottom[0]):
-            part = rows[x * bottom[1] : (x + 1) * bottom[1]]
-            shift = (first_part + x) * bottom[2]
-            packed += pltpu.roll(part, shift, 1) if shift else part
+    def into_message(rows):
+        packed = rows[:second2]
+        for x in range(1, first2):
+            packed += pltpu.roll(rows[x * second2 : (x + 1) * second2], x * width2, 1)
         return packed
 
+    def line(a, which, gath):
+        piece = {
+            "gz": gath.at[me["gx"], me["gy"], me["gz"]],
+            "gx": gath.at[me["gx"], me["gy"]],
+            "gy": gath.at[:, me["gy"]],
+        }[a]
+        base = {"gz": 0, "gx": nz - 1, "gy": nz + nx - 2}[a]
+        return [
+            pltpu.make_async_remote_copy(
+                src_ref=piece,
+                dst_ref=piece,
+                send_sem=gsend.at[which, base + k - 1],
+                recv_sem=grecv.at[which, base + k - 1],
+                device_id={a: lax.rem(me[a] + k, count[a])},
+                device_id_type=MESH,
+            )
+            for k in range(1, count[a])
+        ]
+
+    def begin(copies):
+        for copy in copies:
+            copy.start()
+
+    def finish(copies):
+        for copy in copies:
+            copy.wait_recv()
+        for copy in copies:
+            copy.wait_send()
+
+    def place(gath, ref):
+        lane = lanes_of((second2, LANES))
+
+        @pl.loop(0, nx * nz // 2)
+        def _(n):
+            for m in (2 * n, 2 * n + 1):
+                ix = m // nz
+                iz = m % nz
+                held = [gath[ix, iy, iz] for iy in range(ny)]
+                for x in range(first2):
+                    tile = jnp.zeros((second2, LANES), jnp.float32)
+                    for iy in range(ny):
+                        shift = (iy - x) * width2 % LANES
+                        moved = pltpu.roll(held[iy], shift, 1) if shift else held[iy]
+                        tile = jnp.where(lane // width2 == iy, moved, tile)
+                    start_row = pl.multiple_of(iz * second2, second2)
+                    ref[ix * first2 + x, pl.ds(start_row, second2), :] = tile
+
     def coarsen():
-        for level in range(1, LEVELS):
-            rows = restrict(lambda x: coefs[level - 1][x], blocks[level - 1])
-            spread(rows, blocks[level], coefs[level])
-        rows = restrict(lambda x: coefs[LEVELS - 1][x], blocks[LEVELS - 1])
-        message[...] = into_message(rows, bottom[0])
-
-    for level in range(LEVELS):
-        smooth(level, sources[level], coefs[level], coarsen if level == 0 else lambda: None)
-        resid = level_refs[level][6]
-        rows = restrict(lambda x: resid[x], blocks[level])
-        if level + 1 < LEVELS:
-            spread(rows, blocks[level + 1], sources[level + 1])
-    message[...] += into_message(rows, 0)
-
-    pieces = {
-        "gz": message,
-        "gx": gath.at[me["gx"], me["gy"]],
-        "gy": gath.at[:, me["gy"]],
-    }
-    base = 0
+        spread(restrict(lambda x: ab[x], blocks[0]), blocks[1], coef1)
+        rows = restrict(lambda x: coef1[x], blocks[1])
+        gath_c[me["gx"], me["gy"], me["gz"]] = into_message(rows)
+        begin(line("gz", 0, gath_c))
+
+    def coarse_x():
+        finish(line("gz", 0, gath_c))
+        begin(line("gx", 0, gath_c))
+
+    def coarse_y():
+        finish(line("gx", 0, gath_c))
+        begin(line("gy", 0, gath_c))
+
+    def coarse_all():
+        finish(line("gy", 0, gath_c))
+        place(gath_c, coef2)
+
+    def coarse_bottom():
+        spread(restrict(lambda x: coef2[x], whole2), whole3, coef3)
+
+    fetches[0].wait()
+    smooth(0, rs, ab, {0: coarsen, 1: coarse_x, 2: coarse_y})
+    resid = level_refs[0][6]
+    spread(restrict(lambda x: resid[x], blocks[0]), blocks[1], source1)
+    smooth(1, source1, coef1, {0: coarse_all, 1: coarse_bottom})
+    rows = restrict(lambda x: level_refs[1][6][x], blocks[1])
+
+    gath_s[me["gx"], me["gy"], me["gz"]] = into_message(rows)
     for a in ("gz", "gx", "gy"):
-        made = []
-        for k in range(1, count[a]):
-            made.append(
-                pltpu.make_async_remote_copy(
-                    src_ref=pieces[a],
-                    dst_ref=pieces[a],
-                    send_sem=gsend.at[base],
-                    recv_sem=grecv.at[base],
-                    device_id={a: lax.rem(me[a] + k, count[a])},
-                    device_id_type=MESH,
-                )
-            )
-            base += 1
-        for copy in made:
-            copy.start()
-        for copy in made:
-            copy.wait_recv()
-        for copy in made:
-            copy.wait_send()
-
-    bx, bz, by = bottom
-    whole_x, whole_z, whole_y = bx * nx, bz * nz, by * ny
-    lane = lanes_of((bz, LANES))
-
-    def place(n, carry):
-        ix = n // nz
-        iz = n % nz
-        for part, ref in ((0, src3), (bx, coef3)):
-            for x in range(bx):
-                tile = jnp.zeros((bz, LANES), jnp.float32)
-                for iy in range(ny):
-                    shift = (iy - part - x) * by % LANES
-                    moved = gath[ix, iy, iz]
-                    if shift:
-                        moved = pltpu.roll(moved, shift, 1)
-                    tile = jnp.where(lane // by == iy, moved, tile)
-                ref[ix * bx + x, pl.ds(pl.multiple_of(iz * bz, bz), bz), :] = tile
-        return carry
-
-    lax.fori_loop(0, nx * nz, place, 0)
-
-    upper = smooth_top + 4.0**LEVELS * absorb_top
-    scale = cheb_tables(BOTTOM_ITERS, bottom_low, upper)[0]
+        begin(line(a, 1, gath_s))
+        if a == "gz":
+            width1 = blocks[1][2]
+            for x in range(blocks[1][0]):
+                out1[x] = level_refs[1][7][x][:, :width1]
+        finish(line(a, 1, gath_s))
+    place(gath_s, src2)
+
+    def neighbour_sum(below, d, above, width):
+        second = d.shape[0]
+        lane = lanes_of(d.shape)
+        near = below + above
+        up = pltpu.roll(d, 1, 0)
+        down = pltpu.roll(d, second - 1, 0)
+        up = jnp.concatenate((jnp.where(edge_row == 0, 0.0, up[:8]), up[8:]), 0)
+        down = jnp.concatenate(
+            (down[: second - 8], jnp.where(edge_row == 7, 0.0, down[second - 8 :])), 0
+        )
+        near += up + down
+        left = pltpu.roll(d, 1, 1)
+        right = pltpu.roll(d, LANES - 1, 1)
+        if width == LANES:
+            near += jnp.where(lane == 0, 0.0, left) + jnp.where(lane == LANES - 1, 0.0, right)
+            return near
+        return jnp.where(lane < width, near + left + right, 0.0)
+
+    total_x, total_z, total_y = whole2
+    zero = jnp.zeros((total_z, LANES), jnp.float32)
+    scale, firsts, seconds = cheb_tables(
+        DEGREE + 1, smooth_low, smooth_top + 4.0 ** (LEVELS - 1) * absorb_top
+    )
+    for slot in range(2):
+        dir2[slot, 0] = zero
+        dir2[slot, total_x + 1] = zero
+    chunk = max(1, min(total_x, 256 // total_z))
+
+    @pl.loop(0, total_x // chunk)
+    def _(n):
+        fields = [src2[n * chunk + j] * scale for j in range(chunk)]
+        for j in range(chunk):
+            dir2[0, n * chunk + j + 1] = fields[j]
+            it2[n * chunk + j] = fields[j]
+
+    for r in range(DEGREE + 1):
+        old, new = r % 2, (r + 1) % 2
+
+        @pl.loop(0, total_x // chunk)
+        def _(n, r=r, old=old, new=new):
+            xs = [n * chunk + j for j in range(chunk)]
+            layers = [dir2[old, xs[0] + j] for j in range(chunk + 2)]
+            bases = [(src2 if r in (0, DEGREE) else res2)[x] for x in xs]
+            parts = [coef2[x] for x in xs]
+            results = []
+            for j in range(chunk):
+                near = neighbour_sum(layers[j], layers[j + 1], layers[j + 2], total_y)
+                results.append(bases[j] - ((6.0 + parts[j]) * layers[j + 1] - near))
+            if r < DEGREE:
+                fields = [
+                    firsts[r] * layers[j + 1] + seconds[r] * results[j] for j in range(chunk)
+                ]
+                totals = [it2[x] + d for x, d in zip(xs, fields)]
+                for j, x in enumerate(xs):
+                    it2[x] = totals[j]
+                    dir2[new, x + 1] = totals[j] if r == DEGREE - 1 else fields[j]
+            for j, x in enumerate(xs):
+                res2[x] = results[j]
+
+    spread(restrict(lambda x: res2[x], whole2), whole3, src3)
+
+    whole_x, whole_z, whole_y = whole3
     zero = jnp.zeros((whole_z, LANES), jnp.float32)
-    row = rows_of((whole_z, LANES))
-    lane = lanes_of((whole_z, LANES))
     for ref in (dir3, it3):
         ref[0] = zero
         ref[whole_x + 1] = zero
     for x in range(whole_x):
         source = src3[x]
         res3[x] = source
-        dir3[x + 1] = source * scale
-        it3[x + 1] = source * scale
+        dir3[x + 1] = source * bottom_scale
+        it3[x + 1] = source * bottom_scale
 
     def bottom_turn(n, carry):
         one = tab[0, n]
         two = tab[1, n]
         layers = [dir3[x] for x in range(whole_x + 2)]
+        bases = [res3[x] for x in range(whole_x)]
         for x in range(whole_x):
-            d = layers[x + 1]
-            near = layers[x] + layers[x + 2]
-            near += jnp.where(row == 0, 0.0, pltpu.roll(d, 1, 0))
-            near += jnp.where(row == whole_z - 1, 0.0, pltpu.roll(d, whole_z - 1, 0))
-            if whole_y < LANES:
-                near += pltpu.roll(d, 1, 1) + pltpu.roll(d, LANES - 1, 1)
-                near = jnp.where(lane < whole_y, near, 0.0)
-            else:
-                near += jnp.where(lane == 0, 0.0, pltpu.roll(d, 1, 1))
-                near += jnp.where(lane == LANES - 1, 0.0, pltpu.roll(d, LANES - 1, 1))
-            res = res3[x] - ((6.0 + coef3[x]) * d - near)
+            near = neighbour_sum(layers[x], layers[x + 1], layers[x + 2], whole_y)
+            res = bases[x] - ((6.0 + coef3[x]) * layers[x + 1] - near)
+            d = one * layers[x + 1] + two * res
             res3[x] = res
-            d = one * d + two * res
             dir3[x + 1] = d
             it3[x + 1] += d
         return carry
 
     lax.fori_loop(0, BOTTOM_ITERS - 1, bottom_turn, 0)
 
-    first, second, width = blocks[-1]
     i = lanes_of((LANES, LANES))
     along_y = jnp.where(
-        i < width, trilinear(rows_of((LANES, LANES)), me["gy"] * width + i), 0.0
+        i < width2, trilinear(rows_of((LANES, LANES)), me["gy"] * width2 + i), 0.0
     )
     along_z = trilinear(
-        lanes_of((second, whole_z)), me["gz"] * second + rows_of((second, whole_z))
+        lanes_of((second2, whole_z)), me["gz"] * second2 + rows_of((second2, whole_z))
     )
     layers = []
-    for x in range(first):
-        centre = me["gx"] * (first // 2) + x // 2 + 1
+    for x in range(first2):
+        centre = me["gx"] * (first2 // 2) + x // 2 + 1
         layers.append(0.75 * it3[centre] + 0.25 * it3[centre + 2 * (x % 2) - 1])
     moved = exact_dot(jnp.concatenate(layers, axis=0), along_y)
-    iterate = level_refs[-1][7]
-    for x in range(first):
+    own_rows = pl.ds(pl.multiple_of(me["gz"] * second2, second2), second2)
+    back = lax.rem(LANES - me["gy"] * width2, LANES)
+    for x in range(first2):
         fine = exact_dot(along_z, moved[x * whole_z : (x + 1) * whole_z])
-        out2[x] = (iterate[x] + fine)[:, :width]
-
-    first, second, width = blocks[1]
-    for x in range(first):
-        out1[x] = level_refs[1][7][x][:, :width]
-
-    for level in range(LEVELS):
+        own = pltpu.roll(it2[me["gx"] * first2 + x, own_rows, :], back, 1)
+        out2[x] = (own + fine)[:, :width2]
+
+    for level in range(SPLIT):
         for r in range(DEGREE + 1):
             sent(level, r)
 
@@ -451,7 +537,7 @@
     blocks = [tuple(s // 2**k for s in right_side.shape) for k in range(LEVELS)]
     rounds = DEGREE + 1
     scratch = []
-    for first, second, width in blocks:
+    for first, second, width in blocks[:SPLIT]:
         scratch += [
             pltpu.VMEM((rounds, first + 2, second, LANES), jnp.float32),
             pltpu.VMEM((rounds, 2, first, LANES), jnp.float32),
@@ -463,37 +549,45 @@
             pltpu.VMEM((first, second, LANES), jnp.float32),
             pltpu.VMEM((2, first, second, LANES), jnp.float32),
         ]
-    bx, bz, by = (s // 2 for s in blocks[-1])
-    whole = (bx * nx, bz * nz, LANES)
-    padded = (bx * nx + 2, bz * nz, LANES)
+    first2, second2, _ = blocks[2]
+    x2, z2 = first2 * nx, second2 * nz
+    x3, z3 = x2 // 2, z2 // 2
+    pair_rows = max(blocks[0][0] // 2 * blocks[0][1], x2 // 2 * z2)
     lines = nx + ny + nz - 3
     scratch += [
-        pltpu.VMEM((blocks[0][0] // 2 * blocks[0][1], LANES), jnp.float32),
-        pltpu.VMEM((nx, ny, nz, bz, LANES), jnp.float32),
-        pltpu.VMEM(whole, jnp.float32),
-        pltpu.VMEM(whole, jnp.float32),
-        pltpu.VMEM(padded, jnp.float32),
-        pltpu.VMEM(whole, jnp.float32),
-        pltpu.VMEM(padded, jnp.float32),
-        pltpu.SemaphoreType.DMA((LEVELS * rounds, 6)),
-        pltpu.SemaphoreType.DMA((LEVELS * rounds, 6)),
-        pltpu.SemaphoreType.DMA((lines,)),
-        pltpu.SemaphoreType.DMA((lines,)),
+        pltpu.VMEM(right_side.shape, jnp.float32),
+        pltpu.VMEM(right_side.shape, jnp.float32),
+        pltpu.VMEM((pair_rows, LANES), jnp.float32),
+        pltpu.VMEM((nx, ny, nz, second2, LANES), jnp.float32),
+        pltpu.VMEM((nx, ny, nz, second2, LANES), jnp.float32),
+        pltpu.VMEM((x2, z2, LANES), jnp.float32),
+        pltpu.VMEM((x2, z2, LANES), jnp.float32),
+        pltpu.VMEM((2, x2 + 2, z2, LANES), jnp.float32),
+        pltpu.VMEM((x2, z2, LANES), jnp.float32),
+        pltpu.VMEM((x2, z2, LANES), jnp.float32),
+        pltpu.VMEM((x3, z3, LANES), jnp.float32),
+        pltpu.VMEM((x3, z3, LANES), jnp.float32),
+        pltpu.VMEM((x3 + 2, z3, LANES), jnp.float32),
+        pltpu.VMEM((x3, z3, LANES), jnp.float32),
+        pltpu.VMEM((x3 + 2, z3, LANES), jnp.float32),
+        pltpu.SMEM((2, BOTTOM_ITERS - 1), jnp.float32),
+        pltpu.SemaphoreType.DMA((SPLIT * rounds, 6)),
+        pltpu.SemaphoreType.DMA((SPLIT * rounds, 6)),
+        pltpu.SemaphoreType.DMA((2, lines)),
+        pltpu.SemaphoreType.DMA((2, lines)),
+        pltpu.SemaphoreType.DMA((2,)),
     ]
-    upper = smooth_top + 4.0**LEVELS * absorb_top
-    _, firsts, seconds = cheb_tables(BOTTOM_ITERS, bottom_low, upper)
-    table = jnp.asarray([firsts, seconds], jnp.float32)
     vmem = pl.BlockSpec(memory_space=pltpu.VMEM)
     return pl.pallas_call(
         functools.partial(kernel, sizes, blocks),
         out_shape=tuple(jax.ShapeDtypeStruct(b, jnp.float32) for b in blocks),
-        in_specs=[pl.BlockSpec(memory_space=pltpu.SMEM), vmem, vmem],
+        in_specs=[pl.BlockSpec(memory_space=pl.ANY)] * 2,
         out_specs=(vmem, vmem, vmem),
         scratch_shapes=scratch,
         compiler_params=pltpu.CompilerParams(
             collective_id=0, has_side_effects=True, vmem_limit_bytes=48 * 1024 * 1024
         ),
-    )(table, right_side, absorption)
+    )(right_side, absorption)
 
 
 def solution(mesh):

time: 75.4 us -> 61 us (0.81)
  Pallas kernels: 69.7 us -> 55.9 us
    pallas_call x1, Pallas kernels: 69.7 us -> 55.9 us  [on_device(): pl.pallas_call(functools.partial(kernel, sizes, blocks), out_shape=tuple(...]
    unnamed x9 -> x7, local copies, waits for them, and re-layouts: 4.82 us -> 4.14 us
where the time goes in v3:
time: 61 us; the launch traced here: 60.7 us
  Pallas kernels  55.9 us (92%)
  local copies, waits for them, and re-layouts  4.14 us (7%)
  between operations  0.65 us (1%)
    pallas_call x1, Pallas kernels, on_device(): pl.pallas_call(functools.partial(kernel, sizes, blocks), out_shape=tuple(...  55.9 us
    unnamed x7, local copies, waits for them, and re-layouts  4.14 us

profile of v3, /device:TPU:0, one launch (start us, length us, event | category | flops | bytes accessed | tf_op | source)
XLA Modules:
  0.0 60.7 jit_solution(16472601712238618353)
XLA Ops:
  0.6 0.0 copy-start
  0.6 1.0 %copy-done = f32[16,64,128]{2,1,0:T(8,128)S(1)} copy-done((f32[16,64,128]{2,1,0:T(8,128)S(1)}, f32[16,64,128]{2,1,0:T(8,128)}, u32[]{:S(2)}) %copy-start) | copy-done | bytes 524312
  1.7 0.0 copy-start.1
  1.7 1.0 %copy-done.1 = f32[16,64,128]{2,1,0:T(8,128)S(1)} copy-done((f32[16,64,128]{2,1,0:T(8,128)S(1)}, f32[16,64,128]{2,1,0:T(8,128)}, u32[]{:S(2)}) %copy-start.1) | copy-done | bytes 524312
  2.7 55.9 %shard_map.49 = (f32[16,64,128]{2,1,0:T(8,128)S(1)}, f32[8,32,64]{2,1,0:T(8,128)S(1)}, f32[4,16,32]{2,1,0:T(8,128)S(1)}) custom-call(f32[16,64,128]{2,1,0:T(8,128)S(1)} %copy-done, f32[16,64,128]{2,1,0:T(8,128)S(1)} %copy-done.1), custom_call_target="tpu_custom_call" | custom-call | tf_op jit(solution)/shard_map/pallas_call | solution.py:581
  58.6 0.8 %copy.8 = f32[16,64,128]{2,1,0:T(8,128)} copy(f32[16,64,128]{2,1,0:T(8,128)S(1)} %get-tuple-element.6) | data formatting | bytes 1048576
  59.4 0.7 %copy.9 = f32[8,32,64]{2,1,0:T(8,128)} copy(f32[8,32,64]{2,1,0:T(8,128)S(1)} %get-tuple-element.7) | data formatting | bytes 131072
  60.1 0.6 %copy.10 = f32[4,16,32]{2,1,0:T(8,128)} copy(f32[4,16,32]{2,1,0:T(8,128)S(1)} %get-tuple-element.8) | data formatting | bytes 16384
Async XLA Ops:
  0.6 1.0 %copy-start = (f32[16,64,128]{2,1,0:T(8,128)S(1)}, f32[16,64,128]{2,1,0:T(8,128)}, u32[]{:S(2)}) copy-start(f32[16,64,128]{2,1,0:T(8,128)} %rs_hbm.1) | copy-start | bytes 1572868
  1.7 1.0 %copy-start.1 = (f32[16,64,128]{2,1,0:T(8,128)S(1)}, f32[16,64,128]{2,1,0:T(8,128)}, u32[]{:S(2)}) copy-start(f32[16,64,128]{2,1,0:T(8,128)} %ab_hbm.1) | copy-start | bytes 1572868

commit v4 on v3

--- a/solution.py
+++ b/solution.py
@@ -94,18 +94,17 @@
         tab[0, n] = jnp.float32(firsts[n])
         tab[1, n] = jnp.float32(seconds[n])
 
+    z_peers = [{"gz": k} for k in range(1, nz)]
+    plane_peers = [
+        {"gx": i, "gy": j} for i in range(nx) for j in range(ny) if (i, j) != (0, 0)
+    ]
+
+    def device(offsets):
+        return {a: lax.rem(me[a] + k, count[a]) for a, k in offsets.items()}
+
     barrier = pltpu.get_barrier_semaphore()
-    greeted = 0
-    for a in AXES:
-        for k in range(1, count[a]):
-            pl.semaphore_signal(
-                barrier,
-                inc=1,
-                device_id={a: lax.rem(me[a] + k, count[a])},
-                device_id_type=MESH,
-            )
-            greeted += 1
-    pl.semaphore_wait(barrier, greeted)
+    for peer in z_peers + plane_peers:
+        pl.semaphore_signal(barrier, inc=1, device_id=device(peer), device_id_type=MESH)
 
     half = halving()
 
@@ -161,17 +160,24 @@
             )
         return made
 
-    def start(level, r):
-        for sends, _, copy in copies(level, r):
+    def start(level, r, part):
+        for sends, _, copy in copies(level, r)[part]:
             pl.when(sends)(copy.start)
+
+    along_x, along_zy = slice(0, 2), slice(2, 6)
 
     def arrive(level, r):
         for _, gets, copy in copies(level, r):
             pl.when(gets)(copy.wait_recv)
 
-    def sent(level, r):
-        for sends, _, copy in copies(level, r):
-            pl.when(sends)(copy.wait_send)
+    def all_sent():
+        rounds = [copies(level, r) for level in range(SPLIT) for r in range(DEGREE + 1)]
+        for way in range(6):
+
+            @pl.when(rounds[0][way][0])
+            def _(way=way):
+                for made in rounds:
+                    made[way][2].wait_send()
 
     def put_faces(level, r, x, field, packed):
         second, width = blocks[level][1:]
@@ -186,16 +192,27 @@
         high = pltpu.roll(field, 2 * x + LANES + 1 - width, 1)
         return jnp.where(lane == 2 * x + 1, low, jnp.where(lane == 2 * x, high, packed))
 
-    def by_chunks(level, body, carry):
+    def by_chunks(level, body, carry, ends_done=None):
         first, second, _ = blocks[level]
         chunk = min(first, 256 // second)
+        turns = first // chunk
 
         def turn(n, carry):
-            return body([n * chunk + j for j in range(chunk)], carry)
-
-        if chunk == first:
-            return turn(0, carry)
-        return lax.fori_loop(0, first // chunk, turn, carry)
+            if turns > 2:
+                chosen = jnp.where(n == 0, 0, jnp.where(n == 1, turns - 1, n - 1))
+            else:
+                chosen = n
+            carry = body([chosen * chunk + j for j in range(chunk)], carry)
+            if ends_done is not None and turns > 1:
+                pl.when(n == 1)(ends_done)
+            return carry
+
+        if turns == 1:
+            carry = turn(0, carry)
+            if ends_done is not None:
+                ends_done()
+            return carry
+        return lax.fori_loop(0, turns, turn, carry)
 
     edge_row = rows_of((8, LANES))
 
@@ -285,8 +302,11 @@
             return packed
 
         faces_y[0] = by_chunks(level, opening, empty)
+        if level == 0:
+            pl.semaphore_wait(barrier, len(z_peers) + len(plane_peers))
+        start(level, 0, along_x)
         for r in range(DEGREE + 1):
-            start(level, r)
+            start(level, r, along_zy)
             if level == 0 and r == 0:
                 fetches[1].wait()
             inside(level, r, source if r in (0, DEGREE) else resid, coef)
@@ -318,7 +338,9 @@
             if r == DEGREE:
                 by_chunks(level, last, 0)
             else:
-                faces_y[r + 1] = by_chunks(level, turn, empty)
+                faces_y[r + 1] = by_chunks(
+                    level, turn, empty, lambda r=r: start(level, r + 1, along_x)
+                )
 
     coef1, source1 = level_refs[1][8].at[0], level_refs[1][8].at[1]
     first2, second2, width2 = blocks[2]
@@ -335,23 +357,25 @@
             packed += pltpu.roll(rows[x * second2 : (x + 1) * second2], x * width2, 1)
         return packed
 
-    def line(a, which, gath):
-        piece = {
-            "gz": gath.at[me["gx"], me["gy"], me["gz"]],
-            "gx": gath.at[me["gx"], me["gy"]],
-            "gy": gath.at[:, me["gy"]],
-        }[a]
-        base = {"gz": 0, "gx": nz - 1, "gy": nz + nx - 2}[a]
+    def line(which, gath):
+        piece = gath.at[me["gx"], me["gy"], me["gz"]]
+        return gather(piece, which, z_peers, 0)
+
+    def plane(which, gath):
+        piece = gath.at[me["gx"], me["gy"]]
+        return gather(piece, which, plane_peers, len(z_peers))
+
+    def gather(piece, which, peers, base):
         return [
             pltpu.make_async_remote_copy(
                 src_ref=piece,
                 dst_ref=piece,
-                send_sem=gsend.at[which, base + k - 1],
-                recv_sem=grecv.at[which, base + k - 1],
-                device_id={a: lax.rem(me[a] + k, count[a])},
+                send_sem=gsend.at[which, base + k],
+                recv_sem=grecv.at[which, base + k],
+                device_id=device(peer),
                 device_id_type=MESH,
             )
-            for k in range(1, count[a])
+            for k, peer in enumerate(peers)
         ]
 
     def begin(copies):
@@ -386,38 +410,35 @@
         spread(restrict(lambda x: ab[x], blocks[0]), blocks[1], coef1)
         rows = restrict(lambda x: coef1[x], blocks[1])
         gath_c[me["gx"], me["gy"], me["gz"]] = into_message(rows)
-        begin(line("gz", 0, gath_c))
-
-    def coarse_x():
-        finish(line("gz", 0, gath_c))
-        begin(line("gx", 0, gath_c))
-
-    def coarse_y():
-        finish(line("gx", 0, gath_c))
-        begin(line("gy", 0, gath_c))
+        begin(line(0, gath_c))
+
+    def coarse_plane():
+        finish(line(0, gath_c))
+        begin(plane(0, gath_c))
 
     def coarse_all():
-        finish(line("gy", 0, gath_c))
+        finish(plane(0, gath_c))
         place(gath_c, coef2)
 
     def coarse_bottom():
         spread(restrict(lambda x: coef2[x], whole2), whole3, coef3)
 
     fetches[0].wait()
-    smooth(0, rs, ab, {0: coarsen, 1: coarse_x, 2: coarse_y})
+    smooth(0, rs, ab, {0: coarsen})
     resid = level_refs[0][6]
     spread(restrict(lambda x: resid[x], blocks[0]), blocks[1], source1)
-    smooth(1, source1, coef1, {0: coarse_all, 1: coarse_bottom})
+    smooth(1, source1, coef1, {0: coarse_plane, 3: coarse_all, 4: coarse_bottom})
     rows = restrict(lambda x: level_refs[1][6][x], blocks[1])
 
     gath_s[me["gx"], me["gy"], me["gz"]] = into_message(rows)
-    for a in ("gz", "gx", "gy"):
-        begin(line(a, 1, gath_s))
-        if a == "gz":
-            width1 = blocks[1][2]
-            for x in range(blocks[1][0]):
-                out1[x] = level_refs[1][7][x][:, :width1]
-        finish(line(a, 1, gath_s))
+    begin(line(1, gath_s))
+    width1 = blocks[1][2]
+    for x in range(blocks[1][0]):
+        out1[x] = level_refs[1][7][x][:, :width1]
+    finish(line(1, gath_s))
+    begin(plane(1, gath_s))
+    all_sent()
+    finish(plane(1, gath_s))
     place(gath_s, src2)
 
     def neighbour_sum(below, d, above, width):
@@ -526,10 +547,6 @@
         fine = exact_dot(along_z, moved[x * whole_z : (x + 1) * whole_z])
         own = pltpu.roll(it2[me["gx"] * first2 + x, own_rows, :], back, 1)
         out2[x] = (own + fine)[:, :width2]
-
-    for level in range(SPLIT):
-        for r in range(DEGREE + 1):
-            sent(level, r)
 
 
 def on_device(sizes, right_side, absorption):
@@ -553,7 +570,7 @@
     x2, z2 = first2 * nx, second2 * nz
     x3, z3 = x2 // 2, z2 // 2
     pair_rows = max(blocks[0][0] // 2 * blocks[0][1], x2 // 2 * z2)
-    lines = nx + ny + nz - 3
+    lines = nz - 1 + nx * ny - 1
     scratch += [
         pltpu.VMEM(right_side.shape, jnp.float32),
         pltpu.VMEM(right_side.shape, jnp.float32),
@@ -581,11 +598,11 @@
     return pl.pallas_call(
         functools.partial(kernel, sizes, blocks),
         out_shape=tuple(jax.ShapeDtypeStruct(b, jnp.float32) for b in blocks),
-        in_specs=[pl.BlockSpec(memory_space=pl.ANY)] * 2,
+        in_specs=[pl.BlockSpec(memory_space=pltpu.HBM)] * 2,
         out_specs=(vmem, vmem, vmem),
         scratch_shapes=scratch,
         compiler_params=pltpu.CompilerParams(
-            collective_id=0, has_side_effects=True, vmem_limit_bytes=48 * 1024 * 1024
+            collective_id=0, has_side_effects=True, vmem_limit_bytes=63 * 1024 * 1024
         ),
     )(right_side, absorption)
 

time: 61 us -> 57.1 us (0.936)
  Pallas kernels: 55.9 us -> 52.9 us
  local copies, waits for them, and re-layouts: 4.14 us -> 3.3 us
    pallas_call x1, Pallas kernels: 55.9 us -> 52.9 us  [on_device(): pl.pallas_call(functools.partial(kernel, sizes, blocks), out_shape=tuple(...]
    unnamed x7, local copies, waits for them, and re-layouts: 4.14 us -> 3.3 us
where the time goes in v4:
time: 57.1 us; the launch traced here: 56.9 us
  Pallas kernels  52.9 us (93%)
  local copies, waits for them, and re-layouts  3.3 us (6%)
  between operations  0.65 us (1%)
    pallas_call x1, Pallas kernels, on_device(): pl.pallas_call(functools.partial(kernel, sizes, blocks), out_shape=tuple(...  52.9 us
    unnamed x7, local copies, waits for them, and re-layouts  3.3 us

profile of v4, /device:TPU:0, one launch (start us, length us, event | category | flops | bytes accessed | tf_op | source)
XLA Modules:
  0.0 56.9 jit_solution(11858032913440585941)
XLA Ops:
  0.6 52.9 %shard_map.49 = (f32[16,64,128]{2,1,0:T(8,128)}, f32[8,32,64]{2,1,0:T(8,128)}, f32[4,16,32]{2,1,0:T(8,128)}) custom-call(f32[16,64,128]{2,1,0:T(8,128)} %rs_hbm.1, f32[16,64,128]{2,1,0:T(8,128)} %ab_hbm.1), custom_call_target="tpu_custom_call" | custom-call | tf_op jit(solution)/shard_map/pallas_call | solution.py:598
  53.6 0.0 copy-start
  53.6 1.9 %copy.8 = f32[16,64,128]{2,1,0:T(8,128)} copy(f32[16,64,128]{2,1,0:T(8,128)} %get-tuple-element.6) | data formatting | bytes 1048576
  55.5 0.0 copy-done
  55.5 0.0 copy-start.1
  55.5 0.7 %copy.9 = f32[8,32,64]{2,1,0:T(8,128)} copy(f32[8,32,64]{2,1,0:T(8,128)S(1)} %copy-done) | data formatting | bytes 131072
  56.2 0.1 copy-done.1
  56.3 0.6 %copy.10 = f32[4,16,32]{2,1,0:T(8,128)} copy(f32[4,16,32]{2,1,0:T(8,128)S(1)} %copy-done.1) | data formatting | bytes 16384
Async XLA Ops:
  53.6 1.9 %copy-start = (f32[8,32,64]{2,1,0:T(8,128)S(1)}, f32[8,32,64]{2,1,0:T(8,128)}, u32[]{:S(2)}) copy-start(f32[8,32,64]{2,1,0:T(8,128)} %get-tuple-element.7) | copy-start | bytes 196612
  55.5 0.8 %copy-start.1 = (f32[4,16,32]{2,1,0:T(8,128)S(1)}, f32[4,16,32]{2,1,0:T(8,128)}, u32[]{:S(2)}) copy-start(f32[4,16,32]{2,1,0:T(8,128)} %get-tuple-element.8) | copy-start | bytes 24580

commit v5 on v4

--- a/solution.py
+++ b/solution.py
@@ -87,12 +87,15 @@
     for fetch in fetches:
         fetch.start()
 
-    bottom_scale, firsts, seconds = cheb_tables(
-        BOTTOM_ITERS, bottom_low, smooth_top + 4.0**LEVELS * absorb_top
-    )
-    for n in range(BOTTOM_ITERS - 1):
-        tab[0, n] = jnp.float32(firsts[n])
-        tab[1, n] = jnp.float32(seconds[n])
+    scales = []
+    for level in range(LEVELS + 1):
+        turns, lower = (BOTTOM_ITERS, bottom_low) if level == LEVELS else (DEGREE + 1, smooth_low)
+        scale, firsts, seconds = cheb_tables(turns, lower, smooth_top + 4.0**level * absorb_top)
+        scales.append(scale)
+        for n in range(turns - 1):
+            tab[2 * level, n] = jnp.float32(firsts[n])
+            tab[2 * level + 1, n] = jnp.float32(seconds[n])
+    bottom_scale = scales[LEVELS]
 
     z_peers = [{"gz": k} for k in range(1, nz)]
     plane_peers = [
@@ -283,12 +286,11 @@
 
         return add
 
-    def smooth(level, source, coef, between):
+    def smooth(level, source, coef, between, last_work=None):
         first, second, width = blocks[level]
         dirs, _, faces_y = level_refs[level][:3]
         resid, iterate = level_refs[level][6:8]
-        upper = smooth_top + 4.0**level * absorb_top
-        scale, firsts, seconds = cheb_tables(DEGREE + 1, smooth_low, upper)
+        scale = scales[level]
         empty = jnp.zeros((second, LANES), jnp.float32)
         for r in range(DEGREE + 1):
             dirs[r, 0] = empty
@@ -298,6 +300,7 @@
             fields = [source[x] * scale for x in xs]
             for x, d in zip(xs, fields):
                 iterate[x] = d
+                resid[x] = source[x]
                 packed = put_faces(level, 0, x, d, packed)
             return packed
 
@@ -305,42 +308,49 @@
         if level == 0:
             pl.semaphore_wait(barrier, len(z_peers) + len(plane_peers))
         start(level, 0, along_x)
-        for r in range(DEGREE + 1):
+        if level == 0:
+            fetches[1].wait()
+
+        @pl.loop(0, DEGREE)
+        def _(r):
+            one = tab[2 * level, r]
+            two = tab[2 * level + 1, r]
             start(level, r, along_zy)
-            if level == 0 and r == 0:
-                fetches[1].wait()
-            inside(level, r, source if r in (0, DEGREE) else resid, coef)
-            if r in between:
-                between[r]()
+            inside(level, r, resid, coef)
+            for when, work in between.items():
+                pl.when(r == when)(work)
             arrive(level, r)
             add = outside(level, r)
 
-            def last(xs, carry, add=add):
+            def turn(xs, packed):
                 results = [add(x) for x in xs]
-                for x, res in zip(xs, results):
-                    resid[x] = res
-                return carry
-
-            def turn(xs, packed, r=r, add=add):
-                results = [add(x) for x in xs]
-                fields = [
-                    firsts[r] * dirs[r, x + 1] + seconds[r] * res for x, res in zip(xs, results)
-                ]
+                fields = [one * dirs[r, x + 1] + two * res for x, res in zip(xs, results)]
                 totals = [iterate[x] + d for x, d in zip(xs, fields)]
                 for x, res, d, total in zip(xs, results, fields, totals):
                     resid[x] = res
                     iterate[x] = total
-                    packed = put_faces(
-                        level, r + 1, x, total if r == DEGREE - 1 else d, packed
-                    )
+                    sent = jnp.where(r == DEGREE - 1, total, d)
+                    packed = put_faces(level, r + 1, x, sent, packed)
                 return packed
 
-            if r == DEGREE:
-                by_chunks(level, last, 0)
-            else:
-                faces_y[r + 1] = by_chunks(
-                    level, turn, empty, lambda r=r: start(level, r + 1, along_x)
-                )
+            faces_y[r + 1] = by_chunks(
+                level, turn, empty, lambda: start(level, r + 1, along_x)
+            )
+
+        start(level, DEGREE, along_zy)
+        inside(level, DEGREE, source, coef)
+        if last_work is not None:
+            last_work()
+        arrive(level, DEGREE)
+        add = outside(level, DEGREE)
+
+        def last(xs, carry):
+            results = [add(x) for x in xs]
+            for x, res in zip(xs, results):
+                resid[x] = res
+            return carry
+
+        by_chunks(level, last, 0)
 
     coef1, source1 = level_refs[1][8].at[0], level_refs[1][8].at[1]
     first2, second2, width2 = blocks[2]
@@ -427,7 +437,7 @@
     smooth(0, rs, ab, {0: coarsen})
     resid = level_refs[0][6]
     spread(restrict(lambda x: resid[x], blocks[0]), blocks[1], source1)
-    smooth(1, source1, coef1, {0: coarse_plane, 3: coarse_all, 4: coarse_bottom})
+    smooth(1, source1, coef1, {0: coarse_plane, 3: coarse_all}, coarse_bottom)
     rows = restrict(lambda x: level_refs[1][6][x], blocks[1])
 
     gath_s[me["gx"], me["gy"], me["gz"]] = into_message(rows)
@@ -461,9 +471,7 @@
 
     total_x, total_z, total_y = whole2
     zero = jnp.zeros((total_z, LANES), jnp.float32)
-    scale, firsts, seconds = cheb_tables(
-        DEGREE + 1, smooth_low, smooth_top + 4.0 ** (LEVELS - 1) * absorb_top
-    )
+    scale = scales[LEVELS - 1]
     for slot in range(2):
         dir2[slot, 0] = zero
         dir2[slot, total_x + 1] = zero
@@ -475,30 +483,41 @@
         for j in range(chunk):
             dir2[0, n * chunk + j + 1] = fields[j]
             it2[n * chunk + j] = fields[j]
-
-    for r in range(DEGREE + 1):
-        old, new = r % 2, (r + 1) % 2
+            res2[n * chunk + j] = src2[n * chunk + j]
+
+    def whole_turn(r, base, store):
+        old = lax.rem(r, 2)
 
         @pl.loop(0, total_x // chunk)
-        def _(n, r=r, old=old, new=new):
+        def _(n):
             xs = [n * chunk + j for j in range(chunk)]
             layers = [dir2[old, xs[0] + j] for j in range(chunk + 2)]
-            bases = [(src2 if r in (0, DEGREE) else res2)[x] for x in xs]
+            bases = [base[x] for x in xs]
             parts = [coef2[x] for x in xs]
             results = []
             for j in range(chunk):
                 near = neighbour_sum(layers[j], layers[j + 1], layers[j + 2], total_y)
                 results.append(bases[j] - ((6.0 + parts[j]) * layers[j + 1] - near))
-            if r < DEGREE:
-                fields = [
-                    firsts[r] * layers[j + 1] + seconds[r] * results[j] for j in range(chunk)
-                ]
-                totals = [it2[x] + d for x, d in zip(xs, fields)]
-                for j, x in enumerate(xs):
-                    it2[x] = totals[j]
-                    dir2[new, x + 1] = totals[j] if r == DEGREE - 1 else fields[j]
+            store(xs, layers, results)
             for j, x in enumerate(xs):
                 res2[x] = results[j]
+
+    @pl.loop(0, DEGREE)
+    def _(r):
+        one = tab[2 * LEVELS - 2, r]
+        two = tab[2 * LEVELS - 1, r]
+        new = lax.rem(r + 1, 2)
+
+        def store(xs, layers, results):
+            fields = [one * layers[j + 1] + two * results[j] for j in range(chunk)]
+            totals = [it2[x] + d for x, d in zip(xs, fields)]
+            for j, x in enumerate(xs):
+                it2[x] = totals[j]
+                dir2[new, x + 1] = jnp.where(r == DEGREE - 1, totals[j], fields[j])
+
+        whole_turn(r, res2, store)
+
+    whole_turn(jnp.int32(DEGREE), src2, lambda xs, layers, results: None)
 
     spread(restrict(lambda x: res2[x], whole2), whole3, src3)
 
@@ -514,8 +533,8 @@
         it3[x + 1] = source * bottom_scale
 
     def bottom_turn(n, carry):
-        one = tab[0, n]
-        two = tab[1, n]
+        one = tab[2 * LEVELS, n]
+        two = tab[2 * LEVELS + 1, n]
         layers = [dir3[x] for x in range(whole_x + 2)]
         bases = [res3[x] for x in range(whole_x)]
         for x in range(whole_x):
@@ -587,7 +606,7 @@
         pltpu.VMEM((x3 + 2, z3, LANES), jnp.float32),
         pltpu.VMEM((x3, z3, LANES), jnp.float32),
         pltpu.VMEM((x3 + 2, z3, LANES), jnp.float32),
-        pltpu.SMEM((2, BOTTOM_ITERS - 1), jnp.float32),
+        pltpu.SMEM((2 * LEVELS + 2, BOTTOM_ITERS - 1), jnp.float32),
         pltpu.SemaphoreType.DMA((SPLIT * rounds, 6)),
         pltpu.SemaphoreType.DMA((SPLIT * rounds, 6)),
         pltpu.SemaphoreType.DMA((2, lines)),

time: 57.1 us -> 57.2 us (level)
  no operation moved by 1% of the time
where the time goes in v5:
time: 57.2 us; the launch traced here: 57 us
  Pallas kernels  53 us (93%)
  local copies, waits for them, and re-layouts  3.3 us (6%)
  between operations  0.65 us (1%)
    pallas_call x1, Pallas kernels, on_device(): pl.pallas_call(functools.partial(kernel, sizes, blocks), out_shape=tuple(...  53 us
    unnamed x7, local copies, waits for them, and re-layouts  3.3 us

profile of v5, /device:TPU:0, one launch (start us, length us, event | category | flops | bytes accessed | tf_op | source)
XLA Modules:
  0.0 57.0 jit_solution(11111503319848946137)
XLA Ops:
  0.6 53.0 %shard_map.49 = (f32[16,64,128]{2,1,0:T(8,128)}, f32[8,32,64]{2,1,0:T(8,128)}, f32[4,16,32]{2,1,0:T(8,128)}) custom-call(f32[16,64,128]{2,1,0:T(8,128)} %rs_hbm.1, f32[16,64,128]{2,1,0:T(8,128)} %ab_hbm.1), custom_call_target="tpu_custom_call" | custom-call | tf_op jit(solution)/shard_map/pallas_call | solution.py:617
  53.7 0.0 copy-start
  53.7 1.9 %copy.8 = f32[16,64,128]{2,1,0:T(8,128)} copy(f32[16,64,128]{2,1,0:T(8,128)} %get-tuple-element.6) | data formatting | bytes 1048576
  55.6 0.0 copy-done
  55.6 0.0 copy-start.1
  55.6 0.7 %copy.9 = f32[8,32,64]{2,1,0:T(8,128)} copy(f32[8,32,64]{2,1,0:T(8,128)S(1)} %copy-done) | data formatting | bytes 131072
  56.3 0.1 copy-done.1
  56.4 0.6 %copy.10 = f32[4,16,32]{2,1,0:T(8,128)} copy(f32[4,16,32]{2,1,0:T(8,128)S(1)} %copy-done.1) | data formatting | bytes 16384
Async XLA Ops:
  53.7 1.9 %copy-start = (f32[8,32,64]{2,1,0:T(8,128)S(1)}, f32[8,32,64]{2,1,0:T(8,128)}, u32[]{:S(2)}) copy-start(f32[8,32,64]{2,1,0:T(8,128)} %get-tuple-element.7) | copy-start | bytes 196612
  55.6 0.8 %copy-start.1 = (f32[4,16,32]{2,1,0:T(8,128)S(1)}, f32[4,16,32]{2,1,0:T(8,128)}, u32[]{:S(2)}) copy-start(f32[4,16,32]{2,1,0:T(8,128)} %get-tuple-element.8) | copy-start | bytes 24580

commit v6 on v4

--- a/solution.py
+++ b/solution.py
@@ -74,11 +74,10 @@
 
     per_level = 9
     level_refs = [list(scratch[per_level * k : per_level * (k + 1)]) for k in range(SPLIT)]
-    level_refs[0][7] = out0
     rest = scratch[per_level * SPLIT :]
     rs, ab, pairs, gath_s, gath_c, src2, coef2, dir2, res2, it2 = rest[:10]
     src3, coef3, dir3, res3, it3, tab = rest[10:16]
-    send_sem, recv_sem, gsend, grecv, fetch_sem = rest[16:]
+    send_sem, recv_sem, gsend, grecv, fetch_sem, narrow = rest[16:]
 
     fetches = [
         pltpu.make_async_copy(rs_hbm, rs, fetch_sem.at[0]),
@@ -192,9 +191,9 @@
         high = pltpu.roll(field, 2 * x + LANES + 1 - width, 1)
         return jnp.where(lane == 2 * x + 1, low, jnp.where(lane == 2 * x, high, packed))
 
-    def by_chunks(level, body, carry, ends_done=None):
+    def by_chunks(level, body, carry, ends_done=None, rows=256):
         first, second, _ = blocks[level]
-        chunk = min(first, 256 // second)
+        chunk = min(first, rows // second)
         turns = first // chunk
 
         def turn(n, carry):
@@ -245,7 +244,7 @@
                 resid[x] = results[j]
             return carry
 
-        by_chunks(level, body, 0)
+        by_chunks(level, body, 0, rows=512)
 
     def outside(level, r):
         first, second, width = blocks[level]
@@ -391,9 +390,9 @@
     def place(gath, ref):
         lane = lanes_of((second2, LANES))
 
-        @pl.loop(0, nx * nz // 2)
+        @pl.loop(0, nx * nz // 4)
         def _(n):
-            for m in (2 * n, 2 * n + 1):
+            for m in [4 * n + k for k in range(4)]:
                 ix = m // nz
                 iz = m % nz
                 held = [gath[ix, iy, iz] for iy in range(ny)]
@@ -425,6 +424,8 @@
 
     fetches[0].wait()
     smooth(0, rs, ab, {0: coarsen})
+    keep0 = pltpu.make_async_copy(level_refs[0][7], out0, fetch_sem.at[2])
+    keep0.start()
     resid = level_refs[0][6]
     spread(restrict(lambda x: resid[x], blocks[0]), blocks[1], source1)
     smooth(1, source1, coef1, {0: coarse_plane, 3: coarse_all, 4: coarse_bottom})
@@ -434,7 +435,9 @@
     begin(line(1, gath_s))
     width1 = blocks[1][2]
     for x in range(blocks[1][0]):
-        out1[x] = level_refs[1][7][x][:, :width1]
+        narrow[x] = level_refs[1][7][x][:, :width1]
+    keep1 = pltpu.make_async_copy(narrow, out1, fetch_sem.at[3])
+    keep1.start()
     finish(line(1, gath_s))
     begin(plane(1, gath_s))
     all_sent()
@@ -547,6 +550,8 @@
         fine = exact_dot(along_z, moved[x * whole_z : (x + 1) * whole_z])
         own = pltpu.roll(it2[me["gx"] * first2 + x, own_rows, :], back, 1)
         out2[x] = (own + fine)[:, :width2]
+    keep0.wait()
+    keep1.wait()
 
 
 def on_device(sizes, right_side, absorption):
@@ -592,14 +597,16 @@
         pltpu.SemaphoreType.DMA((SPLIT * rounds, 6)),
         pltpu.SemaphoreType.DMA((2, lines)),
         pltpu.SemaphoreType.DMA((2, lines)),
-        pltpu.SemaphoreType.DMA((2,)),
+        pltpu.SemaphoreType.DMA((4,)),
+        pltpu.VMEM(blocks[1], jnp.float32),
     ]
     vmem = pl.BlockSpec(memory_space=pltpu.VMEM)
+    hbm = pl.BlockSpec(memory_space=pltpu.HBM)
     return pl.pallas_call(
         functools.partial(kernel, sizes, blocks),
         out_shape=tuple(jax.ShapeDtypeStruct(b, jnp.float32) for b in blocks),
-        in_specs=[pl.BlockSpec(memory_space=pltpu.HBM)] * 2,
-        out_specs=(vmem, vmem, vmem),
+        in_specs=[hbm, hbm],
+        out_specs=(hbm, hbm, vmem),
         scratch_shapes=scratch,
         compiler_params=pltpu.CompilerParams(
             collective_id=0, has_side_effects=True, vmem_limit_bytes=63 * 1024 * 1024

time: 57.1 us -> 57 us (level)
  no operation moved by 1% of the time
where the time goes in v6:
time: 57 us; the launch traced here: 56.8 us
  Pallas kernels  52.8 us (93%)
  local copies, waits for them, and re-layouts  3.3 us (6%)
  between operations  0.65 us (1%)
    pallas_call x1, Pallas kernels, on_device(): pl.pallas_call(functools.partial(kernel, sizes, blocks), out_shape=tuple(...  52.8 us
    unnamed x7, local copies, waits for them, and re-layouts  3.3 us

profile of v6, /device:TPU:0, one launch (start us, length us, event | category | flops | bytes accessed | tf_op | source)
XLA Modules:
  0.0 56.8 jit_solution(6157261118601679449)
XLA Ops:
  0.6 52.8 %shard_map.49 = (f32[16,64,128]{2,1,0:T(8,128)}, f32[8,32,64]{2,1,0:T(8,128)}, f32[4,16,32]{2,1,0:T(8,128)}) custom-call(f32[16,64,128]{2,1,0:T(8,128)} %rs_hbm.1, f32[16,64,128]{2,1,0:T(8,128)} %ab_hbm.1), custom_call_target="tpu_custom_call" | custom-call | tf_op jit(solution)/shard_map/pallas_call | solution.py:605
  53.4 0.0 copy-start
  53.5 1.9 %copy.8 = f32[16,64,128]{2,1,0:T(8,128)} copy(f32[16,64,128]{2,1,0:T(8,128)} %get-tuple-element.6) | data formatting | bytes 1048576
  55.4 0.0 copy-done
  55.4 0.0 copy-start.1
  55.4 0.7 %copy.9 = f32[8,32,64]{2,1,0:T(8,128)} copy(f32[8,32,64]{2,1,0:T(8,128)S(1)} %copy-done) | data formatting | bytes 131072
  56.0 0.1 copy-done.1
  56.1 0.6 %copy.10 = f32[4,16,32]{2,1,0:T(8,128)} copy(f32[4,16,32]{2,1,0:T(8,128)S(1)} %copy-done.1) | data formatting | bytes 16384
Async XLA Ops:
  53.4 1.9 %copy-start = (f32[8,32,64]{2,1,0:T(8,128)S(1)}, f32[8,32,64]{2,1,0:T(8,128)}, u32[]{:S(2)}) copy-start(f32[8,32,64]{2,1,0:T(8,128)} %get-tuple-element.7) | copy-start | bytes 196612
  55.4 0.8 %copy-start.1 = (f32[4,16,32]{2,1,0:T(8,128)S(1)}, f32[4,16,32]{2,1,0:T(8,128)}, u32[]{:S(2)}) copy-start(f32[4,16,32]{2,1,0:T(8,128)} %get-tuple-element.8) | copy-start | bytes 24580

commit v7 on v6

--- a/solution.py
+++ b/solution.py
@@ -244,7 +244,7 @@
                 resid[x] = results[j]
             return carry
 
-        by_chunks(level, body, 0, rows=512)
+        by_chunks(level, body, 0)
 
     def outside(level, r):
         first, second, width = blocks[level]
@@ -407,6 +407,8 @@
 
     def coarsen():
         spread(restrict(lambda x: ab[x], blocks[0]), blocks[1], coef1)
+
+    def coarsen_again():
         rows = restrict(lambda x: coef1[x], blocks[1])
         gath_c[me["gx"], me["gy"], me["gz"]] = into_message(rows)
         begin(line(0, gath_c))
@@ -423,7 +425,7 @@
         spread(restrict(lambda x: coef2[x], whole2), whole3, coef3)
 
     fetches[0].wait()
-    smooth(0, rs, ab, {0: coarsen})
+    smooth(0, rs, ab, {0: coarsen, 1: coarsen_again})
     keep0 = pltpu.make_async_copy(level_refs[0][7], out0, fetch_sem.at[2])
     keep0.start()
     resid = level_refs[0][6]

time: 57 us -> 57 us (level)
  no operation moved by 1% of the time
where the time goes in v7:
time: 57 us; the launch traced here: 56.7 us
  Pallas kernels  52.8 us (93%)
  local copies, waits for them, and re-layouts  3.3 us (6%)
  between operations  0.65 us (1%)
    pallas_call x1, Pallas kernels, on_device(): pl.pallas_call(functools.partial(kernel, sizes, blocks), out_shape=tuple(...  52.8 us
    unnamed x7, local copies, waits for them, and re-layouts  3.3 us

profile of v7, /device:TPU:0, one launch (start us, length us, event | category | flops | bytes accessed | tf_op | source)
XLA Modules:
  0.0 56.7 jit_solution(13744598499172663540)
XLA Ops:
  0.6 52.8 %shard_map.49 = (f32[16,64,128]{2,1,0:T(8,128)}, f32[8,32,64]{2,1,0:T(8,128)}, f32[4,16,32]{2,1,0:T(8,128)}) custom-call(f32[16,64,128]{2,1,0:T(8,128)} %rs_hbm.1, f32[16,64,128]{2,1,0:T(8,128)} %ab_hbm.1), custom_call_target="tpu_custom_call" | custom-call | tf_op jit(solution)/shard_map/pallas_call | solution.py:607
  53.4 0.0 copy-start
  53.4 1.9 %copy.8 = f32[16,64,128]{2,1,0:T(8,128)} copy(f32[16,64,128]{2,1,0:T(8,128)} %get-tuple-element.6) | data formatting | bytes 1048576
  55.4 0.0 copy-done
  55.4 0.0 copy-start.1
  55.4 0.7 %copy.9 = f32[8,32,64]{2,1,0:T(8,128)} copy(f32[8,32,64]{2,1,0:T(8,128)S(1)} %copy-done) | data formatting | bytes 131072
  56.0 0.1 copy-done.1
  56.1 0.6 %copy.10 = f32[4,16,32]{2,1,0:T(8,128)} copy(f32[4,16,32]{2,1,0:T(8,128)S(1)} %copy-done.1) | data formatting | bytes 16384
Async XLA Ops:
  53.4 1.9 %copy-start = (f32[8,32,64]{2,1,0:T(8,128)S(1)}, f32[8,32,64]{2,1,0:T(8,128)}, u32[]{:S(2)}) copy-start(f32[8,32,64]{2,1,0:T(8,128)} %get-tuple-element.7) | copy-start | bytes 196612
  55.4 0.8 %copy-start.1 = (f32[4,16,32]{2,1,0:T(8,128)S(1)}, f32[4,16,32]{2,1,0:T(8,128)}, u32[]{:S(2)}) copy-start(f32[4,16,32]{2,1,0:T(8,128)} %get-tuple-element.8) | copy-start | bytes 24580
